TPU v7x, 768 devices: a whole 4x8x12 slice. The times are simulated.
768 devices in a mesh: seq: 96 (over x, z, core), head: 8 (over y).
Axes of the slice: x: 4, y: 8, z: 12, core: 2. Of those that a mesh axis runs over, the one named last changes fastest.
Arguments:
- queries: bfloat16 [12288, 4096], P('seq', 'head'), may hold values from -6 to 6
- keys: bfloat16 [12288, 4096], P('seq', 'head'), may hold values from -6 to 6
- values: bfloat16 [12288, 4096], P('seq', 'head'), may hold values from -3 to 3
- decay_codes: int32 [12288, 32], P('seq', 'head'), may hold values from 0 to 2048
- out_weight: bfloat16 [4096, 3072], P('head'), may hold values from -0.09375 to 0.09375
- out_grad: bfloat16 [12288, 3072], P('seq', 'head'), may hold values from -6 to 6
Outputs:
- mixed: bfloat16 [12288, 3072], P('seq', 'head')
- query_gradient: bfloat16 [12288, 4096], P('seq', 'head')
- key_grad: bfloat16 [12288, 4096], P('seq', 'head')
- value_gradient: bfloat16 [12288, 4096], P('seq', 'head')
All inputs are finite; a program needn't handle non-finite values.
Results may differ from a plain program's by a relative error of at most 0.014.
Values may be sent and summed in bfloat16 or wider, within the bound.
A program may use at most 128 MiB of HBM per device.

v0:
```python
import jax
import jax.numpy as jnp
from jax import lax
from jax.sharding import PartitionSpec as P


def prefix(value, axis, join, neutral):
    count, mine = (lax.axis_size(axis), lax.axis_index(axis))
    pieces = jax.tree.map(lambda part: lax.all_gather(part, axis), value)
    subtotal = jax.tree.map(
        lambda part, zero: jnp.full_like(part, 0) + jnp.asarray(zero, part.dtype), value, neutral
    )

    def prefix_step(position, subtotal):
        longer = join(subtotal, jax.tree.map(lambda part: part[position], pieces))
        return jax.tree.map(lambda new, old: jnp.where(position < mine, new, old), longer, subtotal)

    return lax.fori_loop(0, count - 1, prefix_step, subtotal)


def entering(array, axis, combine, identity):
    devices, place = (lax.axis_size(axis), lax.axis_index(axis))
    everything = jax.tree.map(
        lambda part, kind: lax.all_gather(part.astype(kind), axis),
        array,
        (jnp.bfloat16, jnp.bfloat16),
    )
    start = jax.tree.map(
        lambda part, zero: jnp.broadcast_to(jnp.asarray(zero, part.dtype), part.shape),
        array,
        identity,
    )

    def entering_step(k, before):
        at = devices - 1 - k
        reached = at > place
        new = combine(
            before, jax.tree.map(lambda part, own: part[at].astype(own.dtype), everything, array)
        )
        return jax.tree.map(lambda a, b: jnp.where(reached, a, b), new, before)

    return lax.fori_loop(0, devices, entering_step, start)


def block_mask(cum_log):
    block_len = cum_log.shape[0]
    log_gap = cum_log.T[:, :, None] - cum_log.T[:, None, :]
    lower_part = (jnp.arange(block_len)[:, None] >= jnp.arange(block_len)[None, :])[None]
    return jnp.where(lower_part, jnp.exp(jnp.where(lower_part, log_gap, 0.0)), 0.0)


def combine(earlier, later):
    return (earlier[0] * later[0], later[0][:, None, None] * earlier[1] + later[1])


def local(queries, keys, values, decay_codes, out_weight, out_grad):
    tok_rows = queries.shape[0]
    head_count = decay_codes.shape[1]
    head_width = queries.shape[1] // head_count
    att_scale = 1.0 / head_width
    grad_flat = lax.dot_general(
        lax.all_gather(out_grad, "head", axis=1, tiled=True),
        out_weight,
        (((1,), (1,)), ((), ())),
        preferred_element_type=jnp.float32,
    ).astype(jnp.bfloat16)

    def to_heads(array):
        return array.reshape(tok_rows, head_count, head_width)

    query_h = to_heads(queries)
    key_h = to_heads(keys)
    value_h = to_heads(values)
    grad_h = to_heads(grad_flat)
    cum_log = jnp.cumsum(jnp.log(1.0 - decay_codes.astype(jnp.float32) / 4096.0), axis=0)
    decay_mask = block_mask(cum_log)
    rise_decay = jnp.exp(cum_log)[:, :, None]
    fall_decay = jnp.exp(cum_log[-1][None, :] - cum_log)[:, :, None]
    total_decay = jnp.exp(cum_log[-1])
    k_fall = (fall_decay * key_h.astype(jnp.float32)).astype(jnp.bfloat16)
    summary_fwd = jnp.einsum("thd,the->hde", k_fall, value_h, preferred_element_type=jnp.float32)
    q_rise = (att_scale * rise_decay * query_h.astype(jnp.float32)).astype(jnp.bfloat16)
    summary_bwd = jnp.einsum("shd,she->hde", q_rise, grad_h, preferred_element_type=jnp.float32)
    identity = (
        jnp.ones((head_count,), jnp.float32),
        jnp.zeros((head_count, head_width, head_width), jnp.float32),
    )
    passed_fwd, state_in = prefix((total_decay, summary_fwd), "seq", combine, identity)
    passed_bwd, carry_in = entering((total_decay, summary_bwd), "seq", combine, identity)
    scores = jnp.einsum("she,the->hst", query_h, key_h, preferred_element_type=jnp.float32)
    attn = (att_scale * scores * decay_mask).astype(jnp.bfloat16)
    pscores = jnp.einsum("she,the->hst", grad_h, value_h, preferred_element_type=jnp.float32)
    pmat = (att_scale * pscores * decay_mask).astype(jnp.bfloat16)
    g_rise = (att_scale * rise_decay * grad_h.astype(jnp.float32)).astype(jnp.bfloat16)
    v_fall = (fall_decay * value_h.astype(jnp.float32)).astype(jnp.bfloat16)
    local_out = jnp.einsum("hst,the->she", attn, value_h, preferred_element_type=jnp.float32)
    local_qgrad = jnp.einsum("hst,thd->shd", pmat, key_h, preferred_element_type=jnp.float32)
    local_kgrad = jnp.einsum("hst,shd->thd", pmat, query_h, preferred_element_type=jnp.float32)
    local_vgrad = jnp.einsum("hst,she->the", attn, grad_h, preferred_element_type=jnp.float32)
    state_b = state_in.astype(jnp.bfloat16)
    carry_b = carry_in.astype(jnp.bfloat16)
    attn_out = local_out + jnp.einsum(
        "shd,hde->she", q_rise, state_b, preferred_element_type=jnp.float32
    )
    query_gradient = local_qgrad + jnp.einsum(
        "she,hde->shd", g_rise, state_b, preferred_element_type=jnp.float32
    )
    key_grad = local_kgrad + jnp.einsum(
        "the,hde->thd", v_fall, carry_b, preferred_element_type=jnp.float32
    )
    value_gradient = local_vgrad + jnp.einsum(
        "thd,hde->the", k_fall, carry_b, preferred_element_type=jnp.float32
    )
    attn_flat = attn_out.astype(jnp.bfloat16).reshape(tok_rows, -1)
    partial_out = jnp.dot(attn_flat, out_weight, preferred_element_type=jnp.float32)
    mixed = lax.psum_scatter(
        partial_out.astype(jnp.bfloat16), "head", scatter_dimension=1, tiled=True
    )
    flat_width = queries.shape[1]
    return (
        mixed,
        query_gradient.astype(jnp.bfloat16).reshape(tok_rows, flat_width),
        key_grad.astype(jnp.bfloat16).reshape(tok_rows, flat_width),
        value_gradient.astype(jnp.bfloat16).reshape(tok_rows, flat_width),
    )


def solution(mesh):
    placed = (
        P("seq", "head"),
        P("seq", "head"),
        P("seq", "head"),
        P("seq", "head"),
        P("head", None),
        P("seq", "head"),
    )
    return jax.shard_map(
        local,
        mesh=mesh,
        in_specs=placed,
        out_specs=(P("seq", "head"), P("seq", "head"), P("seq", "head"), P("seq", "head")),
        check_vma=False,
    )
```

profile of v0, /device:TPU:1, one launch (start us, length us, event | category | flops | bytes accessed | tf_op | source)
XLA Modules:
  0.0 614.3 jit_solution(17609907727615442424)
XLA Ops:
  8.5 2.0 fusion.16
  11.7 23.6 %all_gather.26 = bf16[128,3072]{1,0:T(8,128)(2,1)S(1)} all-gather(bf16[128,384]{1,0:T(8,128)(2,1)} %param.15), channel_id=1, replica_groups=mesh['seq'=96,'head'=8] {'head'}, dimensions={1}, use_global_device_ids=true | all-gather | bytes 884736 | tf_op jit(solution)/shard_map/all_gather | solution.py:62
  39.6 1.8 fusion.10
  41.4 1.9 fusion.11
  43.3 1.9 convolution_bitcast_fusion.5
  45.2 1.8 fusion.35
  47.1 77.2 %all-gather.2 = f32[96,1,4]{2,1,0:T(1,128)} all-gather(f32[1,1,4]{2,1,0:T(1,128)S(1)} %get-tuple-element.312), channel_id=1, replica_groups=mesh['seq'=96,'head'=8] {'seq'}, dimensions={0}, use_global_device_ids=true | all-gather | bytes 1552 | tf_op jit(solution)/shard_map/all_gather | solution.py:9
  124.2 1.9 convolution_bitcast_fusion.3
  126.1 58.8 %all-gather.3 = bf16[96,1,4]{2,1,0:T(2,128)(2,1)} all-gather(bf16[1,1,4]{2,1,0:T(2,128)(2,1)S(1)} %get-tuple-element.310), channel_id=1, replica_groups=mesh['seq'=96,'head'=8] {'seq'}, dimensions={0}, use_global_device_ids=true | all-gather | bytes 776 | tf_op jit(solution)/shard_map/all_gather | solution.py:24
  186.6 166.7 %while.30 = (s32[]{:T(128)}, f32[4,128,128]{2,1,0:T(8,128)S(1)}, s32[]{:T(128)}, f32[96,4]{1,0:T(8,128)}, f32[96,4,128,128]{3,2,1,0:T(8,128)}, /*index=5*/s32[]{:T(128)}, s32[]{:T(128)}) while((s32[]{:T(128)}, f32[4,128,128]{2,1,0:T(8,128)S(1)}, s32[]{:T(128)}, f32[96,4]{1,0:T(8,128)}, f32[96,4,128,128]{3,2,1,0:T(8,128)}, ...), condition=%wide.region_2.3_spmd.clone, body=%wide.region_1.2_spmd.clone.sunk | while | flops 262148 | bytes 786593 | solution.py:18
  356.0 2.3 copy.100
  358.3 239.0 %while.31 = (s32[]{:T(128)}, f32[4,128,128]{2,1,0:T(8,128)}, s32[]{:T(128)}, bf16[96,4]{1,0:T(8,128)(2,1)}, bf16[96,4,128,128]{3,2,1,0:T(8,128)(2,1)}, /*index=5*/s32[]{:T(128)}, s32[]{:T(128)}, s32[]{:T(128)}, s32[]{:T(128)}) while((s32[]{:T(128)}, f32[4,128,128]{2,1,0:T(8,128)}, s32[]{:T(128)}, bf16[96,4]{1,0:T(8,128)(2,1)}, ...), condition=%wide.region_5.6_spmd.clone, body=%wide.region_4.5_spmd.clone.sunk | while | flops 327692 | bytes 655575 | solution.py:42
  361.5 1.8 fusion.60
  363.9 1.8 fusion.60
  366.4 1.8 fusion.60
  368.9 1.8 fusion.60
  373.9 1.8 fusion.60
  376.4 1.8 fusion.60
  378.9 1.8 fusion.60
  381.4 1.8 fusion.60
  383.9 1.8 fusion.60
  386.4 1.8 fusion.60
  388.9 1.8 fusion.60
  391.4 1.8 fusion.60
  393.9 1.8 fusion.60
  396.3 1.8 fusion.60
  398.8 1.8 fusion.60
  401.3 1.8 fusion.60
  403.8 1.8 fusion.60
  406.3 1.8 fusion.60
  408.8 1.8 fusion.60
  411.3 1.8 fusion.60
  413.8 1.8 fusion.60
  416.3 1.8 fusion.60
  418.8 1.8 fusion.60
  421.2 1.8 fusion.60
  423.7 1.8 fusion.60
  426.2 1.8 fusion.60
  428.7 1.8 fusion.60
  431.2 1.8 fusion.60
  433.7 1.8 fusion.60
  436.2 1.8 fusion.60
  438.7 1.8 fusion.60
  441.2 1.8 fusion.60
  443.7 1.8 fusion.60
  446.1 1.8 fusion.60
  448.6 1.8 fusion.60
  451.1 1.8 fusion.60
  (388 shorter events, 360.4 us)
Async XLA Ops:
  7.2 28.1 %copy-start = (bf16[512,3072]{1,0:T(8,128)(2,1)S(1)}, bf16[512,3072]{1,0:T(8,128)(2,1)}, u32[]{:S(2)}) copy-start(bf16[512,3072]{1,0:T(8,128)(2,1)} %param.14) | copy-start | bytes 9437188
  7.2 179.4 %all-gather.7.cloned.1.call-start = ((), (), s32[]{:S(2)}) async-start(), calls=%async_computation.1 | async-start | bytes 25427968 | tf_op jit(solution)/shard_map/all_gather | solution.py:9
  8.4 2.2 copy-start.2
  10.5 347.8 %all-gather.9.cloned.1.call-start = ((), (), s32[]{:S(2)}) async-start(), calls=%async_computation.2 | async-start | bytes 12713984 | tf_op jit(solution)/shard_map/all_gather | solution.py:24
  36.6 0.9 copy-start.1
  37.5 568.7 %reduce-scatter.4.cloned.1.call-start = ((), (), s32[]{:S(2)}) async-start(), calls=%async_computation.3 | async-start | bytes 884736
Sparse Core Ops, SparseCore 0:
  11.7 163.1 all-gather.6
  178.6 124.7 all-gather.8
  358.4 32.5 reduce-scatter.3
where the time goes:
time: 625 us; the launch traced here: 614 us
  other arithmetic  340 us (54%)
  blocking collectives  160 us (26%)
  local copies, waits for them, and re-layouts  76.7 us (12%)
  matrix products  21.7 us (3%)
  between operations  13.9 us (2%)
    select_n x96, other arithmetic, entering_step(): return jax.tree.map(lambda a, b: jnp.where(reached, a, b), new, before)  173 us
    select_n x95, other arithmetic, prefix_step(): jnp.where(position < mine, new, old)  99.9 us
    all_gather x1, blocking collectives, prefix(): pieces = jax.tree.map(lambda part: lax.all_gather(part, axis), value)  77.2 us
    convert_element_type x96, other arithmetic, entering_step(): part[at].astype(own.dtype)  65.8 us
    mul x95, local copies, waits for them, and re-layouts, combine(): later[0][:, None, None] * earlier[1] + later[1]  65.1 us
    all_gather x1, blocking collectives, entering(): lax.all_gather(part.astype(kind), axis)  58.8 us
    all_gather x1, blocking collectives, local(): lax.all_gather(out_grad, 'head', axis=1, tiled=True)  23.6 us
  transfers between devices with their start and end apart: 3, of which 0 were waited for; matrix products, arithmetic and copies ran while one was open for 71% of the time, Pallas kernels for 0%

commit v1 on v0

v1 whole, which is shorter than its diff:
```python
import jax
import jax.numpy as jnp
from jax import lax
from jax.experimental import pallas as pl
from jax.experimental.pallas import tpu as pltpu
from jax.sharding import PartitionSpec as P

MESH = pl.DeviceIdType.MESH
BF16 = jnp.bfloat16
F32 = jnp.float32
NX, NZ, NC, NY = 4, 12, 2, 8
ZG = 4
GROUPS = NZ // ZG
MEMBERS = ZG * NC
TOK = 128
HW = 128
NH = 4
COLS = 384
HALF = HW // 2
PIECE = HALF + 16
SCALE = 1.0 / HW


def nn(a, b):
    return lax.dot_general(a, b, (((1,), (0,)), ((), ())), preferred_element_type=F32)


def nt(a, b):
    return lax.dot_general(a, b, (((1,), (1,)), ((), ())), preferred_element_type=F32)


def tn(a, b):
    return lax.dot_general(a, b, (((0,), (0,)), ((), ())), preferred_element_type=F32)


def log_tile(log_total):
    high = log_total.astype(BF16)
    rest = log_total - high.astype(F32)
    mid = rest.astype(BF16)
    low = (rest - mid.astype(F32)).astype(BF16)
    row = lax.broadcasted_iota(jnp.int32, (16, HW), 0)
    parts = [jnp.broadcast_to(part.astype(F32), (16, HW)) for part in (high, mid, low)]
    tile = jnp.where(row == 0, parts[0], jnp.where(row == 1, parts[1], jnp.where(row == 2, parts[2], 0.0)))
    return tile.astype(BF16)


def log_of(piece):
    return jnp.sum(piece[HALF:PIECE].astype(F32), axis=0, keepdims=True)


class Scan:
    def __init__(self, place, reverse, refs):
        self.x, self.z, self.c, self.y = place
        self.reverse = reverse
        (self.psend, self.precv, self.gsend, self.zrecv, self.xsend, self.xrecv, self.bsend, self.brecv,
         self.ps, self.pr, self.zs, self.zr, self.xs, self.xr, self.bs, self.br) = refs
        self.group = self.z // ZG
        self.me = lax.rem(self.z, ZG) * NC + self.c
        self.sent = []

    def device(self, x, z, c):
        return {"seq": x * (NZ * NC) + z * NC + c, "head": self.y}

    def member(self, m):
        return self.device(self.x, self.group * ZG + m // NC, lax.rem(m, NC))

    def copy(self, src, dst, ss, rs, where):
        return pltpu.make_async_remote_copy(src, dst, ss, rs, device_id=where, device_id_type=MESH)

    def put(self, head, summary, log_total):
        tile = log_tile(log_total)
        data = summary.astype(BF16)
        for half in range(2):
            self.psend[2 * head + half, 0:HALF, :] = data[half * HALF:(half + 1) * HALF]
            self.psend[2 * head + half, HALF:PIECE, :] = tile

    def start_pieces(self):
        for k in range(1, MEMBERS):
            to = lax.rem(self.me + k, MEMBERS)
            copy = self.copy(self.psend.at[to], self.precv.at[self.me], self.ps.at[k], self.pr.at[k], self.member(to))
            copy.start()
            self.sent.append(copy)
        self.precv[self.me] = self.psend[self.me]

    def wait_pieces(self):
        for k in range(1, MEMBERS):
            self.sent[k - 1].wait_recv()

    def order(self, count):
        return reversed(range(count)) if self.reverse else range(count)

    def group_total(self):
        total = jnp.zeros((HALF, HW), F32)
        log_total = jnp.zeros((1, HW), F32)
        for m in self.order(MEMBERS):
            piece = self.precv[m]
            log_m = log_of(piece)
            total = jnp.exp(log_m) * total + piece[0:HALF].astype(F32)
            log_total = log_total + log_m
        self.gsend[0:HALF, :] = total.astype(BF16)
        self.gsend[HALF:PIECE, :] = log_tile(log_total)

    def start_groups(self):
        self.zcopies = []
        for k in range(1, GROUPS):
            to = lax.rem(self.group + k, GROUPS)
            copy = self.copy(self.gsend, self.zrecv.at[self.group], self.zs.at[k], self.zr.at[k],
                             self.device(self.x, to * ZG + lax.rem(self.z, ZG), self.c))
            copy.start()
            self.zcopies.append(copy)
        self.zrecv[self.group] = self.gsend[...]

    def prefix(self, recv, count, place):
        before = jnp.zeros((HALF, HW), F32)
        log_before = jnp.zeros((1, HW), F32)
        total = jnp.zeros((HALF, HW), F32)
        log_total = jnp.zeros((1, HW), F32)
        for m in self.order(count):
            before = jnp.where(place == m, total, before)
            log_before = jnp.where(place == m, log_total, log_before)
            piece = recv[m]
            log_m = log_of(piece)
            total = jnp.exp(log_m) * total + piece[0:HALF].astype(F32)
            log_total = log_total + log_m
        return before, log_before, total, log_total

    def wait_groups(self):
        for copy in self.zcopies:
            copy.wait_recv()

    def start_planes(self):
        self.before, self.log_before, total, log_total = self.prefix(self.zrecv, GROUPS, self.group)
        self.xsend[0:HALF, :] = total.astype(BF16)
        self.xsend[HALF:PIECE, :] = log_tile(log_total)
        self.xcopies = []
        for k in range(1, NX):
            to = lax.rem(self.x + k, NX)
            copy = self.copy(self.xsend, self.xrecv.at[self.x], self.xs.at[k], self.xr.at[k],
                             self.device(to, self.z, self.c))
            copy.start()
            self.xcopies.append(copy)
        self.xrecv[self.x] = self.xsend[...]

    def wait_planes(self):
        for copy in self.xcopies:
            copy.wait_recv()

    def start_back(self):
        entering, _, _, _ = self.prefix(self.xrecv, NX, self.x)
        state = jnp.exp(self.log_before) * entering + self.before
        for m in self.order(MEMBERS):
            self.bsend[m] = state.astype(BF16)
            piece = self.precv[m]
            state = jnp.exp(log_of(piece)) * state + piece[0:HALF].astype(F32)
        self.bcopies = []
        rows = pl.ds(pl.multiple_of(self.me * HALF, HALF), HALF)
        for k in range(1, MEMBERS):
            to = lax.rem(self.me + k, MEMBERS)
            copy = self.copy(self.bsend.at[to], self.brecv.at[rows], self.bs.at[k], self.br.at[k], self.member(to))
            copy.start()
            self.bcopies.append(copy)
        self.brecv[rows, :] = self.bsend[self.me]

    def wait_back(self):
        for copy in self.bcopies:
            copy.wait_recv()

    def finish(self):
        for copy in self.sent + self.zcopies + self.xcopies + self.bcopies:
            copy.wait_send()


SCAN_BUFFERS = [
    pltpu.VMEM((MEMBERS, PIECE, HW), BF16),
    pltpu.VMEM((MEMBERS, PIECE, HW), BF16),
    pltpu.VMEM((PIECE, HW), BF16),
    pltpu.VMEM((GROUPS, PIECE, HW), BF16),
    pltpu.VMEM((PIECE, HW), BF16),
    pltpu.VMEM((NX, PIECE, HW), BF16),
    pltpu.VMEM((MEMBERS, HALF, HW), BF16),
    pltpu.VMEM((NH * HW, HW), BF16),
    pltpu.SemaphoreType.DMA((MEMBERS,)),
    pltpu.SemaphoreType.DMA((MEMBERS,)),
    pltpu.SemaphoreType.DMA((GROUPS,)),
    pltpu.SemaphoreType.DMA((GROUPS,)),
    pltpu.SemaphoreType.DMA((NX,)),
    pltpu.SemaphoreType.DMA((NX,)),
    pltpu.SemaphoreType.DMA((MEMBERS,)),
    pltpu.SemaphoreType.DMA((MEMBERS,)),
]
NB = len(SCAN_BUFFERS)


def kernel(q_ref, k_ref, v_ref, codes_ref, w_hbm, og_ref, mixed_ref, qg_ref, kg_ref, vg_ref, *scratch):
    fwd_refs, bwd_refs, rest = scratch[:NB], scratch[NB:2 * NB], scratch[2 * NB:]
    (w_ref, w_sem, ag, ag_ss, ag_rs, rs_send, rs_recv, rs_ss, rs_rs,
     attn_s, kfall_s, qrise_s, grad_s, out_s, qg_s, kg_s, vg_s, rise_s, fall_s) = rest
    seq, y = lax.axis_index("seq"), lax.axis_index("head")
    x, z, c = seq // (NZ * NC), lax.rem(seq, NZ * NC) // NC, lax.rem(seq, NC)
    place = (x, z, c, y)
    fwd, bwd = Scan(place, False, fwd_refs), Scan(place, True, bwd_refs)

    w_copy = pltpu.make_async_copy(w_hbm, w_ref, w_sem)
    w_copy.start()

    def row(offset):
        return {"seq": seq, "head": lax.rem(y + NY + offset, NY)}

    barrier = pltpu.get_barrier_semaphore()
    greeted = [fwd.member(lax.rem(fwd.me + k, MEMBERS)) for k in range(1, MEMBERS)]
    greeted += [fwd.device(x, lax.rem(z + k * ZG, NZ), c) for k in range(1, GROUPS)]
    greeted += [fwd.device(lax.rem(x + k, NX), z, c) for k in range(1, NX)]
    greeted += [row(k) for k in (1, -1, 2, -2)]
    for where in greeted:
        pl.semaphore_signal(barrier, inc=1, device_id=where, device_id_type=MESH)

    rate = 1.0 - codes_ref[...].astype(F32) * (1.0 / 4096.0)
    logs = jnp.log(rate)
    ri = lax.broadcasted_iota(jnp.int32, (TOK, TOK), 0)
    ci = lax.broadcasted_iota(jnp.int32, (TOK, TOK), 1)
    lower = ri >= ci
    log_pad = jnp.zeros((TOK, TOK), F32)
    for h in range(NH):
        log_pad = jnp.where(ci == h, logs[:, h:h + 1], log_pad)
    cum = lax.dot_general(lower.astype(F32), log_pad, (((1,), (0,)), ((), ())),
                          precision=lax.Precision.HIGHEST, preferred_element_type=F32)
    cum_t = cum.T
    heads = [slice(h * HW, (h + 1) * HW) for h in range(NH)]
    for h in range(NH):
        column = jnp.broadcast_to(cum[:, h:h + 1], (TOK, HW))
        last = column[TOK - 1:TOK]
        fall = jnp.exp(last - column)
        fall_s[h] = fall
        rise_s[h] = jnp.exp(column) * SCALE
        k_fall = (fall * k_ref[:, heads[h]].astype(F32)).astype(BF16)
        kfall_s[:, heads[h]] = k_fall
        fwd.put(h, tn(k_fall, v_ref[:, heads[h]]), last)

    pl.semaphore_wait(barrier, len(greeted))
    fwd.start_pieces()
    ag_copies = {}
    for i, k in enumerate((2, -2, 1, -1)):
        ag_copies[k] = pltpu.make_async_remote_copy(
            og_ref, ag.at[y], ag_ss.at[i], ag_rs.at[i], device_id=row(k), device_id_type=MESH)
        ag_copies[k].start()

    masks = []
    for h in range(NH):
        column = jnp.broadcast_to(cum[:, h:h + 1], (TOK, TOK))
        gap = column - cum_t[h:h + 1, :]
        mask = jnp.where(lower, jnp.exp(jnp.where(lower, gap, 0.0)), 0.0) * SCALE
        masks.append(mask)
        q_h, k_h, v_h = q_ref[:, heads[h]], k_ref[:, heads[h]], v_ref[:, heads[h]]
        attn = (nt(q_h, k_h) * mask).astype(BF16)
        attn_s[h] = attn
        qrise_s[:, heads[h]] = (rise_s[h] * q_h.astype(F32)).astype(BF16)
        out_s[:, heads[h]] = nn(attn, v_h)

    w_copy.wait()

    def w_cols(owner):
        return w_ref[:, pl.ds(pl.multiple_of(owner * COLS, 128), COLS)]

    grad_s[...] = nt(og_ref[...], w_cols(y))

    def add_grad(offset):
        owner = lax.rem(y + NY + offset, NY)
        grad_s[...] += nt(ag[owner], w_cols(owner))

    for sign, i, rows in ((1, 4, slice(0, HALF)), (-1, 6, slice(HALF, TOK))):
        ag_copies[2 * sign].wait_recv()
        owner = lax.rem(y + NY - 2 * sign, NY)
        ag_copies[4 * sign] = pltpu.make_async_remote_copy(
            ag.at[owner, rows], ag.at[owner, rows], ag_ss.at[i + 1], ag_rs.at[i + 1],
            device_id=row(2 * sign), device_id_type=MESH)
        ag_copies[4 * sign].start()
        ag_copies[3 * sign] = pltpu.make_async_remote_copy(
            ag.at[owner], ag.at[owner], ag_ss.at[i], ag_rs.at[i], device_id=row(sign), device_id_type=MESH)
        ag_copies[3 * sign].start()
    fwd.wait_pieces()
    fwd.group_total()
    fwd.start_groups()
    add_grad(2)
    add_grad(-2)
    for sign in (1, -1):
        ag_copies[sign].wait_recv()
        add_grad(-sign)
    for sign in (1, -1):
        ag_copies[3 * sign].wait_recv()
        add_grad(-3 * sign)
    for sign in (1, -1):
        ag_copies[4 * sign].wait_recv()
    add_grad(4)
    fwd.wait_groups()
    fwd.start_planes()
    for h in range(NH):
        last = jnp.broadcast_to(cum[TOK - 1:TOK, h:h + 1], (1, HW))
        bwd.put(h, tn(qrise_s[:, heads[h]], grad_s[:, heads[h]].astype(BF16)), last)
    bwd.start_pieces()
    fwd.wait_planes()
    fwd.start_back()

    for h in range(NH):
        g_h = grad_s[:, heads[h]].astype(BF16)
        q_h, k_h, v_h = q_ref[:, heads[h]], k_ref[:, heads[h]], v_ref[:, heads[h]]
        pmat = (nt(g_h, v_h) * masks[h]).astype(BF16)
        qg_s[:, heads[h]] = nn(pmat, k_h)
        kg_s[:, heads[h]] = tn(pmat, q_h)
        vg_s[:, heads[h]] = tn(attn_s[h], g_h)

    bwd.wait_pieces()
    bwd.group_total()
    bwd.start_groups()

    fwd.wait_back()
    for h in range(NH):
        out_s[:, heads[h]] += nn(qrise_s[:, heads[h]], fwd.brecv[heads[h], :])
    attn_out = out_s[...].astype(BF16)

    def part(offset):
        return nn(attn_out, w_cols(lax.rem(y + NY + offset, NY)))

    rs = {}

    def send(key, i, src, dst, where):
        rs[key] = pltpu.make_async_remote_copy(
            src, dst, rs_ss.at[i], rs_rs.at[i], device_id=where, device_id_type=MESH)
        rs[key].start()

    rs_send[0] = part(4).astype(BF16)
    send(4, 0, rs_send.at[0, 0:HALF], rs_recv.at[0, 0:HALF], row(2))
    send(-4, 1, rs_send.at[0, HALF:TOK], rs_recv.at[0, HALF:TOK], row(-2))
    for slot, k in ((1, 3), (2, -3)):
        rs_send[slot] = part(k).astype(BF16)
        send(k, 1 + slot, rs_send.at[slot], rs_recv.at[slot], row(1 if k > 0 else -1))
    for slot, k in ((3, 1), (4, -1)):
        rs_send[slot] = part(k).astype(BF16)
        send(k, 1 + slot, rs_send.at[slot], rs_recv.at[slot], row(k))
    onward = {1: part(2), -1: part(-2)}
    own = part(0)

    bwd.wait_groups()
    bwd.start_planes()

    for slot, sign, rows in ((5, 1, slice(0, HALF)), (6, -1, slice(HALF, TOK))):
        rs[3 * sign].wait_recv()
        rs[4 * sign].wait_recv()
        total = onward[sign] + rs_recv[1 if sign > 0 else 2].astype(F32)
        near = rs_recv[0, rows].astype(F32)
        if sign > 0:
            rs_send[slot, 0:HALF] = (total[0:HALF] + near).astype(BF16)
            rs_send[slot, HALF:TOK] = total[HALF:TOK].astype(BF16)
        else:
            rs_send[slot, 0:HALF] = total[0:HALF].astype(BF16)
            rs_send[slot, HALF:TOK] = (total[HALF:TOK] + near).astype(BF16)
        send(2 * sign, 1 + slot, rs_send.at[slot], rs_recv.at[slot], row(2 * sign))

    bwd.wait_planes()
    bwd.start_back()

    for h in range(NH):
        g_rise = (rise_s[h] * grad_s[:, heads[h]].astype(BF16).astype(F32)).astype(BF16)
        qg_ref[:, heads[h]] = (qg_s[:, heads[h]] + nt(g_rise, fwd.brecv[heads[h], :])).astype(BF16)

    for key in (1, -1, 2, -2):
        rs[key].wait_recv()
    total = own
    for slot in (3, 4, 5, 6):
        total = total + rs_recv[slot].astype(F32)
    mixed_ref[...] = total.astype(BF16)

    bwd.wait_back()
    for h in range(NH):
        carry = bwd.brecv[heads[h], :]
        v_fall = (fall_s[h] * v_ref[:, heads[h]].astype(F32)).astype(BF16)
        kg_ref[:, heads[h]] = (kg_s[:, heads[h]] + nt(v_fall, carry)).astype(BF16)
        vg_ref[:, heads[h]] = (vg_s[:, heads[h]] + nn(kfall_s[:, heads[h]], carry)).astype(BF16)

    fwd.finish()
    bwd.finish()
    for copy in list(ag_copies.values()) + list(rs.values()):
        copy.wait_send()


def local(queries, keys, values, decay_codes, out_weight, out_grad):
    vmem = pl.BlockSpec(memory_space=pltpu.VMEM)
    wide = NH * HW
    return pl.pallas_call(
        kernel,
        out_shape=(
            jax.ShapeDtypeStruct((TOK, COLS), BF16),
            jax.ShapeDtypeStruct((TOK, wide), BF16),
            jax.ShapeDtypeStruct((TOK, wide), BF16),
            jax.ShapeDtypeStruct((TOK, wide), BF16),
        ),
        in_specs=[vmem, vmem, vmem, vmem, pl.BlockSpec(memory_space=pl.ANY), vmem],
        out_specs=(vmem,) * 4,
        scratch_shapes=SCAN_BUFFERS + SCAN_BUFFERS + [
            pltpu.VMEM(out_weight.shape, BF16),
            pltpu.SemaphoreType.DMA,
            pltpu.VMEM((NY, TOK, COLS), BF16),
            pltpu.SemaphoreType.DMA((8,)),
            pltpu.SemaphoreType.DMA((8,)),
            pltpu.VMEM((7, TOK, COLS), BF16),
            pltpu.VMEM((7, TOK, COLS), BF16),
            pltpu.SemaphoreType.DMA((8,)),
            pltpu.SemaphoreType.DMA((8,)),
            pltpu.VMEM((NH, TOK, TOK), BF16),
            pltpu.VMEM((TOK, wide), BF16),
            pltpu.VMEM((TOK, wide), BF16),
            pltpu.VMEM((TOK, wide), F32),
            pltpu.VMEM((TOK, wide), F32),
            pltpu.VMEM((TOK, wide), F32),
            pltpu.VMEM((TOK, wide), F32),
            pltpu.VMEM((TOK, wide), F32),
            pltpu.VMEM((NH, TOK, HW), F32),
            pltpu.VMEM((NH, TOK, HW), F32),
        ],
        name="linear_attention",
        compiler_params=pltpu.CompilerParams(
            collective_id=0, has_side_effects=True, vmem_limit_bytes=40 * 1024 * 1024
        ),
    )(queries, keys, values, decay_codes, out_weight, out_grad)


def solution(mesh):
    placed = (
        P("seq", "head"),
        P("seq", "head"),
        P("seq", "head"),
        P("seq", "head"),
        P("head", None),
        P("seq", "head"),
    )
    return jax.shard_map(
        local,
        mesh=mesh,
        in_specs=placed,
        out_specs=(P("seq", "head"), P("seq", "head"), P("seq", "head"), P("seq", "head")),
        check_vma=False,
    )
```

time: 625 us -> 65.6 us (0.10); the launches traced: 614 us -> 65.4 us
  other arithmetic: 340 us -> 0 us
  blocking collectives: 160 us -> 0 us
  local copies, waits for them, and re-layouts: 76.7 us -> 8.88 us
  Pallas kernels: 0 us -> 55.8 us
  matrix products: 21.7 us -> 0 us
  between operations: 13.9 us -> 0.65 us
    select_n x191 -> x0, other arithmetic: 273 us -> none  [the longest x96 173 us: entering_step(): return jax.tree.map(lambda a, b: jnp.where(reached, a, b), new, before)]
    all_gather x3 -> x0, blocking collectives: 160 us -> none  [the longest x1 77.2 us: prefix(): pieces = jax.tree.map(lambda part: lax.all_gather(part, axis), value)]
    convert_element_type x96 -> x0, other arithmetic: 65.8 us -> none  [entering_step(): part[at].astype(own.dtype)]
    mul x96 -> x0, local copies, waits for them, and re-layouts: 65.1 us -> none  [the longest x95 65.1 us: combine(): later[0][:, None, None] * earlier[1] + later[1]]
    pallas_call x0 -> x1, Pallas kernels: none -> 55.8 us  [local(): pl.pallas_call(kernel, out_shape=(jax.ShapeDtypeStruct((TOK, COLS), BF16)...]
    dot_general x14 -> x0, matrix products: 21.7 us -> none  [the longest x1 2.01 us: local(): jnp.einsum('thd,the->hde', k_fall, value_h, preferred_element_type=jnp.fl...]
  transfers between devices with their start and end apart: 3 -> 0, of which waited for: 0 -> 0; matrix products, arithmetic and copies ran while one was open for 71% -> 0% of each run, Pallas kernels for 0% -> 0%
where the time goes in v1:
time: 65.6 us; the launch traced here: 65.4 us
  Pallas kernels  55.8 us (85%)
  local copies, waits for them, and re-layouts  8.88 us (14%)
    pallas_call x1, Pallas kernels, local(): pl.pallas_call(kernel, out_shape=(jax.ShapeDtypeStruct((TOK, COLS), BF16)...  55.8 us
    unnamed x15, local copies, waits for them, and re-layouts  8.88 us

profile of v1, /device:TPU:1, one launch (start us, length us, event | category | flops | bytes accessed | tf_op | source)
XLA Modules:
  0.0 65.4 jit_solution(7352766193405083481)
XLA Ops:
  0.6 0.8 %copy.10.codes_ref = s32[128,4]{1,0:T(8,128)S(1)} copy(s32[128,4]{0,1:T(4,128)} %param.9) | data formatting | bytes 4096 | tf_op args[3]
  1.4 0.0 copy-start
  1.4 1.9 %copy-done = bf16[512,3072]{1,0:T(8,128)(2,1)S(1)} copy-done((bf16[512,3072]{1,0:T(8,128)(2,1)S(1)}, bf16[512,3072]{1,0:T(8,128)(2,1)}, u32[]{:S(2)}) %copy-start) | copy-done | bytes 3145752
  3.3 0.0 copy-start.1
  3.3 0.9 %copy-done.1 = bf16[128,512]{1,0:T(8,128)(2,1)S(1)} copy-done((bf16[128,512]{1,0:T(8,128)(2,1)S(1)}, bf16[128,512]{1,0:T(8,128)(2,1)}, u32[]{:S(2)}) %copy-start.1) | copy-done | bytes 131096
  4.2 0.0 copy-start.2
  4.2 0.9 %copy-done.2 = bf16[128,512]{1,0:T(8,128)(2,1)S(1)} copy-done((bf16[128,512]{1,0:T(8,128)(2,1)S(1)}, bf16[128,512]{1,0:T(8,128)(2,1)}, u32[]{:S(2)}) %copy-start.2) | copy-done | bytes 131096
  5.1 0.0 copy-start.3
  5.1 0.9 %copy-done.3 = bf16[128,512]{1,0:T(8,128)(2,1)S(1)} copy-done((bf16[128,512]{1,0:T(8,128)(2,1)S(1)}, bf16[128,512]{1,0:T(8,128)(2,1)}, u32[]{:S(2)}) %copy-start.3) | copy-done | bytes 131096
  6.0 0.0 copy-start.4
  6.0 0.9 %copy-done.4 = bf16[128,384]{1,0:T(8,128)(2,1)S(1)} copy-done((bf16[128,384]{1,0:T(8,128)(2,1)S(1)}, bf16[128,384]{1,0:T(8,128)(2,1)}, u32[]{:S(2)}) %copy-start.4) | copy-done | bytes 98328
  6.9 55.8 %linear_attention.1 = (bf16[128,384]{1,0:T(8,128)(2,1)S(1)}, bf16[128,512]{1,0:T(8,128)(2,1)S(1)}, bf16[128,512]{1,0:T(8,128)(2,1)S(1)}, bf16[128,512]{1,0:T(8,128)(2,1)S(1)}) custom-call(bf16[128,512]{1,0:T(8,128)(2,1)S(1)} %copy-done.1, bf16[128,512]{1,0:T(8,128)(2,1)S(1)} %copy-done.2, bf16[128,512]{1,0:T(8,128)(2,1)S(1)} %copy-done.3, ...), custom_call_target="tpu_custom_call" | custom-call | tf_op jit(solution)/shard_map/linear_attention/pallas_call | solution.py:388
  62.8 0.6 copy.15
  63.4 0.7 %copy.16 = bf16[128,512]{1,0:T(8,128)(2,1)} copy(bf16[128,512]{1,0:T(8,128)(2,1)S(1)} %get-tuple-element.9) | data formatting | bytes 262144
  64.1 0.7 %copy.17 = bf16[128,512]{1,0:T(8,128)(2,1)} copy(bf16[128,512]{1,0:T(8,128)(2,1)S(1)} %get-tuple-element.10) | data formatting | bytes 262144
  64.7 0.7 %copy.18 = bf16[128,512]{1,0:T(8,128)(2,1)} copy(bf16[128,512]{1,0:T(8,128)(2,1)S(1)} %get-tuple-element.11) | data formatting | bytes 262144
Async XLA Ops:
  1.4 1.9 %copy-start = (bf16[512,3072]{1,0:T(8,128)(2,1)S(1)}, bf16[512,3072]{1,0:T(8,128)(2,1)}, u32[]{:S(2)}) copy-start(bf16[512,3072]{1,0:T(8,128)(2,1)} %w_hbm.1) | copy-start | bytes 9437188
  3.3 0.9 %copy-start.1 = (bf16[128,512]{1,0:T(8,128)(2,1)S(1)}, bf16[128,512]{1,0:T(8,128)(2,1)}, u32[]{:S(2)}) copy-start(bf16[128,512]{1,0:T(8,128)(2,1)} %q_ref.1) | copy-start | bytes 393220
  4.2 0.9 %copy-start.2 = (bf16[128,512]{1,0:T(8,128)(2,1)S(1)}, bf16[128,512]{1,0:T(8,128)(2,1)}, u32[]{:S(2)}) copy-start(bf16[128,512]{1,0:T(8,128)(2,1)} %k_ref.1) | copy-start | bytes 393220
  5.1 0.9 %copy-start.3 = (bf16[128,512]{1,0:T(8,128)(2,1)S(1)}, bf16[128,512]{1,0:T(8,128)(2,1)}, u32[]{:S(2)}) copy-start(bf16[128,512]{1,0:T(8,128)(2,1)} %v_ref.1) | copy-start | bytes 393220
  6.0 0.9 %copy-start.4 = (bf16[128,384]{1,0:T(8,128)(2,1)S(1)}, bf16[128,384]{1,0:T(8,128)(2,1)}, u32[]{:S(2)}) copy-start(bf16[128,384]{1,0:T(8,128)(2,1)} %og_ref.1) | copy-start | bytes 294916

commit v2 on v1

v2 whole, which is shorter than its diff:
```python
import contextlib

import jax
import jax.numpy as jnp
from jax import lax
from jax.experimental import pallas as pl
from jax.experimental.pallas import tpu as pltpu
from jax.sharding import PartitionSpec as P

MESH = pl.DeviceIdType.MESH
BF16 = jnp.bfloat16
F32 = jnp.float32
NX, NZ, NC, NY = 4, 12, 2, 8
ZG = 4
GROUPS = NZ // ZG
MEMBERS = ZG * NC
TOK = 128
HW = 128
NH = 4
COLS = 384
HALF = HW // 2
PIECE = HALF + 16
SCALE = 1.0 / HW
TRACE = False


def scope(name):
    return jax.named_scope(name) if TRACE else contextlib.nullcontext()


def nn(a, b):
    return lax.dot_general(a, b, (((1,), (0,)), ((), ())), preferred_element_type=F32)


def nt(a, b):
    return lax.dot_general(a, b, (((1,), (1,)), ((), ())), preferred_element_type=F32)


def tn(a, b):
    return lax.dot_general(a, b, (((0,), (0,)), ((), ())), preferred_element_type=F32)


def log_tile(log_total):
    high = log_total.astype(BF16)
    rest = log_total - high.astype(F32)
    mid = rest.astype(BF16)
    low = (rest - mid.astype(F32)).astype(BF16)
    row = lax.broadcasted_iota(jnp.int32, (16, HW), 0)
    parts = [jnp.broadcast_to(part.astype(F32), (16, HW)) for part in (high, mid, low)]
    tile = jnp.where(row == 0, parts[0], jnp.where(row == 1, parts[1], jnp.where(row == 2, parts[2], 0.0)))
    return tile.astype(BF16)


def log_of(piece):
    return jnp.sum(piece[HALF:PIECE].astype(F32), axis=0, keepdims=True)


class Scan:
    def __init__(self, place, reverse, refs):
        self.x, self.z, self.c, self.y = place
        self.reverse = reverse
        (self.psend, self.precv, self.gsend, self.zrecv, self.xsend, self.xrecv, self.bsend, self.brecv, self.sem) = refs
        self.group = self.z // ZG
        self.me = lax.rem(self.z, ZG) * NC + self.c

    def device(self, x, z, c):
        return {"seq": x * (NZ * NC) + z * NC + c, "head": self.y}

    def member(self, m):
        return self.device(self.x, self.group * ZG + m // NC, lax.rem(m, NC))

    def copy(self, src, dst, exchange, where):
        return pltpu.make_async_remote_copy(src, dst, self.sem.at[2 * exchange], self.sem.at[2 * exchange + 1],
                                            device_id=where, device_id_type=MESH)

    def all_of(self, exchange):
        ref = (self.precv.at[0:MEMBERS - 1], self.zrecv.at[0:GROUPS - 1], self.xrecv.at[0:NX - 1],
               self.brecv.at[0:(MEMBERS - 1) * HALF])[exchange]
        return self.copy(ref, ref, exchange, self.member(lax.rem(self.me + 1, MEMBERS)))

    def put(self, head, summary, log_total):
        tile = log_tile(log_total)
        data = summary.astype(BF16)
        for half in range(2):
            self.psend[2 * head + half, 0:HALF, :] = data[half * HALF:(half + 1) * HALF]
            self.psend[2 * head + half, HALF:PIECE, :] = tile

    def start_pieces(self):
        for k in (4, 3, 5, 2, 6, 1, 7):
            to = lax.rem(self.me + k, MEMBERS)
            self.copy(self.psend.at[to], self.precv.at[self.me], 0, self.member(to)).start()
        self.precv[self.me] = self.psend[self.me]

    def wait_pieces(self):
        self.all_of(0).wait_recv()

    def order(self, count):
        return reversed(range(count)) if self.reverse else range(count)

    def start_groups(self):
        total = jnp.zeros((HALF, HW), F32)
        log_total = jnp.zeros((1, HW), F32)
        for m in self.order(MEMBERS):
            piece = self.precv[m]
            log_m = log_of(piece)
            total = jnp.exp(log_m) * total + piece[0:HALF].astype(F32)
            log_total = log_total + log_m
        self.gsend[0:HALF, :] = total.astype(BF16)
        self.gsend[HALF:PIECE, :] = log_tile(log_total)
        for k in range(1, GROUPS):
            to = lax.rem(self.group + k, GROUPS)
            self.copy(self.gsend, self.zrecv.at[self.group], 1,
                      self.device(self.x, to * ZG + lax.rem(self.z, ZG), self.c)).start()
        self.zrecv[self.group] = self.gsend[...]

    def prefix(self, recv, count, place):
        before = jnp.zeros((HALF, HW), F32)
        log_before = jnp.zeros((1, HW), F32)
        total = jnp.zeros((HALF, HW), F32)
        log_total = jnp.zeros((1, HW), F32)
        for m in self.order(count):
            before = jnp.where(place == m, total, before)
            log_before = jnp.where(place == m, log_total, log_before)
            piece = recv[m]
            log_m = log_of(piece)
            total = jnp.exp(log_m) * total + piece[0:HALF].astype(F32)
            log_total = log_total + log_m
        return before, log_before, total, log_total

    def wait_groups(self):
        self.all_of(1).wait_recv()

    def start_planes(self):
        self.before, self.log_before, total, log_total = self.prefix(self.zrecv, GROUPS, self.group)
        self.xsend[0:HALF, :] = total.astype(BF16)
        self.xsend[HALF:PIECE, :] = log_tile(log_total)
        for k in (2, 1, 3):
            to = lax.rem(self.x + k, NX)
            self.copy(self.xsend, self.xrecv.at[self.x], 2, self.device(to, self.z, self.c)).start()
        self.xrecv[self.x] = self.xsend[...]

    def wait_planes(self):
        self.all_of(2).wait_recv()

    def start_back(self):
        entering, _, _, _ = self.prefix(self.xrecv, NX, self.x)
        state = jnp.exp(self.log_before) * entering + self.before
        for m in self.order(MEMBERS):
            self.bsend[m] = state.astype(BF16)
            piece = self.precv[m]
            state = jnp.exp(log_of(piece)) * state + piece[0:HALF].astype(F32)
        rows = pl.ds(pl.multiple_of(self.me * HALF, HALF), HALF)
        for k in (4, 3, 5, 2, 6, 1, 7):
            to = lax.rem(self.me + k, MEMBERS)
            self.copy(self.bsend.at[to], self.brecv.at[rows], 3, self.member(to)).start()
        self.brecv[rows, :] = self.bsend[self.me]

    def wait_back(self):
        self.all_of(3).wait_recv()

    def finish(self):
        for exchange in range(4):
            self.all_of(exchange).wait_send()


SCAN_BUFFERS = [
    pltpu.VMEM((MEMBERS, PIECE, HW), BF16),
    pltpu.VMEM((MEMBERS, PIECE, HW), BF16),
    pltpu.VMEM((PIECE, HW), BF16),
    pltpu.VMEM((GROUPS, PIECE, HW), BF16),
    pltpu.VMEM((PIECE, HW), BF16),
    pltpu.VMEM((NX, PIECE, HW), BF16),
    pltpu.VMEM((MEMBERS, HALF, HW), BF16),
    pltpu.VMEM((NH * HW, HW), BF16),
    pltpu.SemaphoreType.DMA((8,)),
]
NB = len(SCAN_BUFFERS)


def kernel(q_hbm, k_hbm, v_hbm, codes_hbm, w_hbm, og_hbm, mixed_out, qg_out, kg_out, vg_out, *scratch):
    fwd_refs, bwd_refs, rest = scratch[:NB], scratch[NB:2 * NB], scratch[2 * NB:]
    (q_ref, k_ref, v_ref, codes_ref, w_ref, og_ref, in_sem, ag, ag_sem, rs_send, rs_recv, rs_sem,
     attn_s, kfall_s, qrise_s, grad_s, out_s, qg_s, kg_s, vg_s, rise_s, fall_s,
     mixed_ref, qg_ref, kg_ref, vg_ref, out_sem) = rest
    seq, y = lax.axis_index("seq"), lax.axis_index("head")
    x, z, c = seq // (NZ * NC), lax.rem(seq, NZ * NC) // NC, lax.rem(seq, NC)
    place = (x, z, c, y)
    fwd, bwd = Scan(place, False, fwd_refs), Scan(place, True, bwd_refs)

    codes_copy, k_copy, v_copy, og_copy, q_copy, w_copy = [
        pltpu.make_async_copy(src, dst, in_sem.at[i])
        for i, (src, dst) in enumerate(((codes_hbm, codes_ref), (k_hbm, k_ref), (v_hbm, v_ref), (og_hbm, og_ref),
                                        (q_hbm, q_ref), (w_hbm, w_ref)))
    ]
    codes_copy.start()

    def row(offset):
        return {"seq": seq, "head": lax.rem(y + NY + offset, NY)}

    barrier = pltpu.get_barrier_semaphore()
    greeted = [fwd.member(lax.rem(fwd.me + k, MEMBERS)) for k in range(1, MEMBERS)]
    greeted += [fwd.device(x, lax.rem(z + k * ZG, NZ), c) for k in range(1, GROUPS)]
    greeted += [fwd.device(lax.rem(x + k, NX), z, c) for k in range(1, NX)]
    greeted += [row(k) for k in (1, -1, 2, -2)]
    for where in greeted:
        pl.semaphore_signal(barrier, inc=1, device_id=where, device_id_type=MESH)
    for copy in (k_copy, v_copy, og_copy, q_copy, w_copy):
        copy.start()

    with scope("wait_codes"):
        codes_copy.wait()
    logs = jnp.log(1.0 - codes_ref[...].astype(F32) * (1.0 / 4096.0))
    ri = lax.broadcasted_iota(jnp.int32, (TOK, TOK), 0)
    ci = lax.broadcasted_iota(jnp.int32, (TOK, TOK), 1)
    lower = ri >= ci
    log_pad = jnp.zeros((TOK, TOK), F32)
    for h in range(NH):
        log_pad = jnp.where(ri == h, logs[h:h + 1, :], log_pad)
    cum_t = lax.dot_general(log_pad, (ri <= ci).astype(F32), (((1,), (0,)), ((), ())),
                            precision=lax.Precision.HIGHEST, preferred_element_type=F32)
    cum = cum_t.T
    with scope("wait_kv"):
        k_copy.wait()
        v_copy.wait()
    heads = [slice(h * HW, (h + 1) * HW) for h in range(NH)]
    for h in range(NH):
        column = jnp.broadcast_to(cum[:, h:h + 1], (TOK, HW))
        last = column[TOK - 1:TOK]
        fall = jnp.exp(last - column)
        fall_s[h] = fall
        rise_s[h] = jnp.exp(column) * SCALE
        k_fall = (fall * k_ref[:, heads[h]].astype(F32)).astype(BF16)
        kfall_s[:, heads[h]] = k_fall
        fwd.put(h, tn(k_fall, v_ref[:, heads[h]]), last)

    with scope("wait_barrier"):
        og_copy.wait()
        pl.semaphore_wait(barrier, len(greeted))
    top, bottom, every = slice(0, HALF), slice(HALF, TOK), slice(0, TOK)

    def ag_copy(owner, rows, i, where, src=None):
        src = ag.at[owner, rows] if src is None else src
        return pltpu.make_async_remote_copy(src, ag.at[owner, rows], ag_sem.at[0], ag_sem.at[i],
                                            device_id=where, device_id_type=MESH)

    def ag_wait(i, owner, rows=every):
        ag_copy(owner, rows, i, row(1)).wait_recv()

    def at(offset):
        return lax.rem(y + NY + offset, NY)

    for i, rows in ((1, top), (3, bottom)):
        for j, sign in enumerate((1, -1)):
            ag_copy(y, rows, i + j, row(2 * sign), og_ref.at[rows]).start()
    fwd.start_pieces()

    q_copy.wait()
    masks = []
    for h in range(NH):
        column = jnp.broadcast_to(cum[:, h:h + 1], (TOK, TOK))
        gap = column - cum_t[h:h + 1, :]
        mask = jnp.where(lower, jnp.exp(jnp.where(lower, gap, 0.0)), 0.0) * SCALE
        masks.append(mask)
        q_h, k_h, v_h = q_ref[:, heads[h]], k_ref[:, heads[h]], v_ref[:, heads[h]]
        attn = (nt(q_h, k_h) * mask).astype(BF16)
        attn_s[h] = attn
        qrise_s[:, heads[h]] = (rise_s[h] * q_h.astype(F32)).astype(BF16)
        out_s[:, heads[h]] = nn(attn, v_h)

    for j, sign in enumerate((1, -1)):
        ag_copy(y, every, 5 + j, row(sign), og_ref).start()
    with scope("wait_w"):
        w_copy.wait()

    def w_cols(owner):
        return w_ref[:, pl.ds(pl.multiple_of(owner * COLS, 128), COLS)]

    grad_s[...] = nt(og_ref[...], w_cols(y))

    def add_grad(offset):
        grad_s[...] += nt(ag[at(offset)], w_cols(at(offset)))

    with scope("wait_pieces_fwd"):
        fwd.wait_pieces()
    fwd.start_groups()
    for i, rows in ((1, top), (3, bottom)):
        for j, sign in enumerate((1, -1)):
            owner = at(-2 * sign)
            with scope("wait_ag2"):
                ag_wait(i + j, owner, rows)
            if (rows == top) == (sign == 1):
                ag_copy(owner, rows, 9, row(2 * sign)).start()
            ag_copy(owner, rows, 7 + j, row(sign)).start()
    add_grad(2)
    add_grad(-2)
    for j, sign in enumerate((1, -1)):
        with scope("wait_ag1"):
            ag_wait(5 + j, at(-sign))
        add_grad(-sign)
    with scope("wait_groups_fwd"):
        fwd.wait_groups()
    fwd.start_planes()
    for j, sign in enumerate((1, -1)):
        with scope("wait_ag3"):
            ag_wait(7 + j, at(-3 * sign))
        add_grad(-3 * sign)
    with scope("wait_ag4"):
        ag_wait(9, at(4))
    add_grad(4)
    for h in range(NH):
        last = jnp.broadcast_to(cum[TOK - 1:TOK, h:h + 1], (1, HW))
        bwd.put(h, tn(qrise_s[:, heads[h]], grad_s[:, heads[h]].astype(BF16)), last)
    bwd.start_pieces()
    with scope("wait_planes_fwd"):
        fwd.wait_planes()
    fwd.start_back()

    for h in range(NH):
        g_h = grad_s[:, heads[h]].astype(BF16)
        q_h, k_h, v_h = q_ref[:, heads[h]], k_ref[:, heads[h]], v_ref[:, heads[h]]
        pmat = (nt(g_h, v_h) * masks[h]).astype(BF16)
        qg_s[:, heads[h]] = nn(pmat, k_h)
        kg_s[:, heads[h]] = tn(pmat, q_h)
        vg_s[:, heads[h]] = tn(attn_s[h], g_h)

    with scope("wait_pieces_bwd"):
        bwd.wait_pieces()
    bwd.start_groups()

    with scope("wait_back_fwd"):
        fwd.wait_back()
    for h in range(NH):
        out_s[:, heads[h]] += nn(qrise_s[:, heads[h]], fwd.brecv[heads[h], :])
    attn_out = out_s[...].astype(BF16)

    def part(offset):
        return nn(attn_out, w_cols(lax.rem(y + NY + offset, NY)))

    out_copies = [pltpu.make_async_copy(src, dst, out_sem.at[i]) for i, (src, dst) in enumerate(
        ((mixed_ref, mixed_out), (qg_ref, qg_out), (kg_ref, kg_out), (vg_ref, vg_out)))]

    def rs_copy(slot, rows, i, where):
        return pltpu.make_async_remote_copy(rs_send.at[slot, rows], rs_recv.at[slot, rows], rs_sem.at[0], rs_sem.at[i],
                                            device_id=where, device_id_type=MESH)

    ways = ((1, bottom, top), (-1, top, bottom))
    for j, (sign, first, second) in enumerate(ways):
        rs_send[j] = part(3 * sign).astype(BF16)
        rs_copy(j, first, 1 + j, row(sign)).start()
    rs_send[2] = part(4).astype(BF16)
    for j, (sign, first, second) in enumerate(ways):
        rs_copy(2, second, 3 + j, row(2 * sign)).start()
        rs_copy(j, second, 3 + j, row(sign)).start()
    for j, (sign, first, second) in enumerate(ways):
        rs_send[3 + j] = part(sign).astype(BF16)
        rs_copy(3 + j, every, 5, row(sign)).start()
    onward = [part(2 * sign) for sign, _, _ in ways]
    own = part(0)

    with scope("wait_groups_bwd"):
        bwd.wait_groups()
    bwd.start_planes()

    for j, (sign, first, second) in enumerate(ways):
        with scope("wait_rs3"):
            rs_copy(j, first, 1 + j, row(sign)).wait_recv()
        rs_send[5 + j, first] = (onward[j][first] + rs_recv[j, first].astype(F32)).astype(BF16)
        rs_copy(5 + j, first, 5, row(2 * sign)).start()
    for j, (sign, first, second) in enumerate(ways):
        with scope("wait_rs4"):
            rs_copy(j, every, 3 + j, row(sign)).wait_recv()
        rs_send[5 + j, second] = (onward[j][second] + rs_recv[j, second].astype(F32)
                                  + rs_recv[2, second].astype(F32)).astype(BF16)
        rs_copy(5 + j, second, 5, row(2 * sign)).start()

    with scope("wait_planes_bwd"):
        bwd.wait_planes()
    bwd.start_back()

    for h in range(NH):
        g_rise = (rise_s[h] * grad_s[:, heads[h]].astype(BF16).astype(F32)).astype(BF16)
        qg_ref[:, heads[h]] = (qg_s[:, heads[h]] + nt(g_rise, fwd.brecv[heads[h], :])).astype(BF16)
    out_copies[1].start()

    with scope("wait_back_bwd"):
        bwd.wait_back()
    for h in range(NH):
        carry = bwd.brecv[heads[h], :]
        v_fall = (fall_s[h] * v_ref[:, heads[h]].astype(F32)).astype(BF16)
        kg_ref[:, heads[h]] = (kg_s[:, heads[h]] + nt(v_fall, carry)).astype(BF16)
        vg_ref[:, heads[h]] = (vg_s[:, heads[h]] + nn(kfall_s[:, heads[h]], carry)).astype(BF16)
    out_copies[2].start()
    out_copies[3].start()

    with scope("wait_rs2"):
        pltpu.make_async_remote_copy(rs_send.at[3:7], rs_recv.at[3:7], rs_sem.at[0], rs_sem.at[5],
                                     device_id=row(1), device_id_type=MESH).wait_recv()
    total = own
    for slot in (3, 4, 5, 6):
        total = total + rs_recv[slot].astype(F32)
    mixed_ref[...] = total.astype(BF16)
    out_copies[0].start()

    with scope("wait_sends"):
        fwd.finish()
        bwd.finish()
        pltpu.make_async_remote_copy(ag.at[0:7], ag.at[0:7], ag_sem.at[0], ag_sem.at[1],
                                     device_id=row(1), device_id_type=MESH).wait_send()
        pltpu.make_async_remote_copy(rs_send, rs_recv, rs_sem.at[0], rs_sem.at[1],
                                     device_id=row(1), device_id_type=MESH).wait_send()
    with scope("wait_out"):
        for copy in out_copies:
            copy.wait()


def store(*refs):
    sources, targets, sem = refs[:4], refs[4:8], refs[8]
    copies = [pltpu.make_async_copy(src, dst, sem.at[i]) for i, (src, dst) in enumerate(zip(sources, targets))]
    for copy in copies:
        copy.start()
    for copy in copies:
        copy.wait()


def local(queries, keys, values, decay_codes, out_weight, out_grad):
    vmem = pl.BlockSpec(memory_space=pltpu.VMEM)
    wide = NH * HW
    placed = [
        pltpu.with_memory_space_constraint(array, pltpu.HBM)
        for array in (queries, keys, values, decay_codes.T, out_weight, out_grad)
    ]
    results = pl.pallas_call(
        kernel,
        out_shape=(
            pltpu.VMEM((TOK, COLS), BF16),
            pltpu.VMEM((TOK, wide), BF16),
            pltpu.VMEM((TOK, wide), BF16),
            pltpu.VMEM((TOK, wide), BF16),
        ),
        in_specs=[pl.BlockSpec(memory_space=pltpu.HBM)] * 6,
        out_specs=(pl.BlockSpec(memory_space=pl.ANY),) * 4,
        scratch_shapes=SCAN_BUFFERS + SCAN_BUFFERS + [
            pltpu.VMEM((TOK, wide), BF16),
            pltpu.VMEM((TOK, wide), BF16),
            pltpu.VMEM((TOK, wide), BF16),
            pltpu.VMEM((NH, TOK), jnp.int32),
            pltpu.VMEM(out_weight.shape, BF16),
            pltpu.VMEM((TOK, COLS), BF16),
            pltpu.SemaphoreType.DMA((6,)),
            pltpu.VMEM((NY, TOK, COLS), BF16),
            pltpu.SemaphoreType.DMA((10,)),
            pltpu.VMEM((7, TOK, COLS), BF16),
            pltpu.VMEM((7, TOK, COLS), BF16),
            pltpu.SemaphoreType.DMA((6,)),
            pltpu.VMEM((NH, TOK, TOK), BF16),
            pltpu.VMEM((TOK, wide), BF16),
            pltpu.VMEM((TOK, wide), BF16),
            pltpu.VMEM((TOK, wide), F32),
            pltpu.VMEM((TOK, wide), F32),
            pltpu.VMEM((TOK, wide), F32),
            pltpu.VMEM((TOK, wide), F32),
            pltpu.VMEM((TOK, wide), F32),
            pltpu.VMEM((NH, TOK, HW), F32),
            pltpu.VMEM((NH, TOK, HW), F32),
            pltpu.VMEM((TOK, COLS), BF16),
            pltpu.VMEM((TOK, wide), BF16),
            pltpu.VMEM((TOK, wide), BF16),
            pltpu.VMEM((TOK, wide), BF16),
            pltpu.SemaphoreType.DMA((4,)),
        ],
        name="linear_attention",
        compiler_params=pltpu.CompilerParams(
            collective_id=0, has_side_effects=True, vmem_limit_bytes=40 * 1024 * 1024
        ),
    )(*placed)
    return pl.pallas_call(
        store,
        out_shape=tuple(jax.ShapeDtypeStruct(array.shape, array.dtype) for array in results),
        in_specs=[vmem] * 4,
        out_specs=tuple([pl.BlockSpec(memory_space=pltpu.HBM)] * 4),
        scratch_shapes=[pltpu.SemaphoreType.DMA((4,))],
        name="store",
    )(*[pltpu.with_memory_space_constraint(array, pltpu.VMEM) for array in results])


def solution(mesh):
    placed = (
        P("seq", "head"),
        P("seq", "head"),
        P("seq", "head"),
        P("seq", "head"),
        P("head", None),
        P("seq", "head"),
    )
    return jax.shard_map(
        local,
        mesh=mesh,
        in_specs=placed,
        out_specs=(P("seq", "head"), P("seq", "head"), P("seq", "head"), P("seq", "head")),
        check_vma=False,
    )
```

time: 65.6 us -> 53.9 us (0.82)
  local copies, waits for them, and re-layouts: 8.88 us -> 0 us
  Pallas kernels: 55.8 us -> 53.2 us
    unnamed x15 -> x0, local copies, waits for them, and re-layouts: 8.88 us -> none
    pallas_call x1 -> x2, Pallas kernels: 55.8 us -> 53.2 us  [the longest x1 52.4 us: local(): pl.pallas_call(kernel, out_shape=(pltpu.VMEM((TOK, COLS), BF16), pltpu.VM...]
where the time goes in v2:
time: 53.9 us; the launch traced here: 53.8 us
  Pallas kernels  53.2 us (99%)
  between operations  0.64 us (1%)
    pallas_call x1, Pallas kernels, local(): pl.pallas_call(kernel, out_shape=(pltpu.VMEM((TOK, COLS), BF16), pltpu.VM...  52.4 us

profile of v2, /device:TPU:1, one launch (start us, length us, event | category | flops | bytes accessed | tf_op | source)
XLA Modules:
  0.0 53.8 jit_solution(13291478851358078233)
XLA Ops:
  0.6 52.4 %linear_attention.1 = (bf16[128,384]{1,0:T(8,128)(2,1)S(1)}, bf16[128,512]{1,0:T(8,128)(2,1)S(1)}, bf16[128,512]{1,0:T(8,128)(2,1)S(1)}, bf16[128,512]{1,0:T(8,128)(2,1)S(1)}) custom-call(bf16[128,512]{1,0:T(8,128)(2,1)} %q_hbm.1, bf16[128,512]{1,0:T(8,128)(2,1)} %k_hbm.1, bf16[128,512]{1,0:T(8,128)(2,1)} %v_hbm.1, s32[4,128]{1,0:T(4,128)} %bitcast.1, ...), custom_call_target="tpu_custom_call" | custom-call | tf_op jit(solution)/shard_map/linear_attention/pallas_call | solution.py:432
  53.0 0.8 %store.1 = (bf16[128,384]{1,0:T(8,128)(2,1)}, bf16[128,512]{1,0:T(8,128)(2,1)}, bf16[128,512]{1,0:T(8,128)(2,1)}, bf16[128,512]{1,0:T(8,128)(2,1)}) custom-call(bf16[128,384]{1,0:T(8,128)(2,1)S(1)} %get-tuple-element.8.refs_0_, bf16[128,512]{1,0:T(8,128)(2,1)S(1)} %get-tuple-element.9.refs_1_, bf16[128,512]{1,0:T(8,128)(2,1)S(1)} %get-tuple-element.10.refs_2_, ...), custom_call_target="tpu_custom_call" | custom-call | tf_op jit(solution)/shard_map/store/pallas_call | solution.py:476

commit v3 on v2

--- a/solution.py
+++ b/solution.py
@@ -21,6 +21,8 @@
 HALF = HW // 2
 PIECE = HALF + 16
 SCALE = 1.0 / HW
+AG_PARTS = 2
+RS_PARTS = 2
 TRACE = False
 
 
@@ -51,14 +53,15 @@
     return tile.astype(BF16)
 
 
-def log_of(piece):
-    return jnp.sum(piece[HALF:PIECE].astype(F32), axis=0, keepdims=True)
+def log_of(ref, m):
+    return jnp.sum(ref[m, HALF:PIECE].astype(F32), axis=0, keepdims=True)
 
 
 class Scan:
-    def __init__(self, place, reverse, refs):
+    def __init__(self, place, reverse, refs, other=None):
         self.x, self.z, self.c, self.y = place
         self.reverse = reverse
+        self.decays = other or self
         (self.psend, self.precv, self.gsend, self.zrecv, self.xsend, self.xrecv, self.bsend, self.brecv, self.sem) = refs
         self.group = self.z // ZG
         self.me = lax.rem(self.z, ZG) * NC + self.c
@@ -79,11 +82,11 @@
         return self.copy(ref, ref, exchange, self.member(lax.rem(self.me + 1, MEMBERS)))
 
     def put(self, head, summary, log_total):
-        tile = log_tile(log_total)
         data = summary.astype(BF16)
         for half in range(2):
             self.psend[2 * head + half, 0:HALF, :] = data[half * HALF:(half + 1) * HALF]
-            self.psend[2 * head + half, HALF:PIECE, :] = tile
+            if self.decays is self:
+                self.psend[2 * head + half, HALF:PIECE, :] = log_tile(log_total)
 
     def start_pieces(self):
         for k in (4, 3, 5, 2, 6, 1, 7):
@@ -101,19 +104,19 @@
         total = jnp.zeros((HALF, HW), F32)
         log_total = jnp.zeros((1, HW), F32)
         for m in self.order(MEMBERS):
-            piece = self.precv[m]
-            log_m = log_of(piece)
-            total = jnp.exp(log_m) * total + piece[0:HALF].astype(F32)
+            log_m = log_of(self.decays.precv, m)
+            total = jnp.exp(log_m) * total + self.precv[m, 0:HALF].astype(F32)
             log_total = log_total + log_m
         self.gsend[0:HALF, :] = total.astype(BF16)
-        self.gsend[HALF:PIECE, :] = log_tile(log_total)
+        if self.decays is self:
+            self.gsend[HALF:PIECE, :] = log_tile(log_total)
         for k in range(1, GROUPS):
             to = lax.rem(self.group + k, GROUPS)
             self.copy(self.gsend, self.zrecv.at[self.group], 1,
                       self.device(self.x, to * ZG + lax.rem(self.z, ZG), self.c)).start()
         self.zrecv[self.group] = self.gsend[...]
 
-    def prefix(self, recv, count, place):
+    def prefix(self, recv, decays, count, place):
         before = jnp.zeros((HALF, HW), F32)
         log_before = jnp.zeros((1, HW), F32)
         total = jnp.zeros((HALF, HW), F32)
@@ -121,9 +124,8 @@
         for m in self.order(count):
             before = jnp.where(place == m, total, before)
             log_before = jnp.where(place == m, log_total, log_before)
-            piece = recv[m]
-            log_m = log_of(piece)
-            total = jnp.exp(log_m) * total + piece[0:HALF].astype(F32)
+            log_m = log_of(decays, m)
+            total = jnp.exp(log_m) * total + recv[m, 0:HALF].astype(F32)
             log_total = log_total + log_m
         return before, log_before, total, log_total
 
@@ -131,9 +133,11 @@
         self.all_of(1).wait_recv()
 
     def start_planes(self):
-        self.before, self.log_before, total, log_total = self.prefix(self.zrecv, GROUPS, self.group)
+        self.before, self.log_before, total, log_total = self.prefix(
+            self.zrecv, self.decays.zrecv, GROUPS, self.group)
         self.xsend[0:HALF, :] = total.astype(BF16)
-        self.xsend[HALF:PIECE, :] = log_tile(log_total)
+        if self.decays is self:
+            self.xsend[HALF:PIECE, :] = log_tile(log_total)
         for k in (2, 1, 3):
             to = lax.rem(self.x + k, NX)
             self.copy(self.xsend, self.xrecv.at[self.x], 2, self.device(to, self.z, self.c)).start()
@@ -143,12 +147,11 @@
         self.all_of(2).wait_recv()
 
     def start_back(self):
-        entering, _, _, _ = self.prefix(self.xrecv, NX, self.x)
+        entering, _, _, _ = self.prefix(self.xrecv, self.decays.xrecv, NX, self.x)
         state = jnp.exp(self.log_before) * entering + self.before
         for m in self.order(MEMBERS):
             self.bsend[m] = state.astype(BF16)
-            piece = self.precv[m]
-            state = jnp.exp(log_of(piece)) * state + piece[0:HALF].astype(F32)
+            state = jnp.exp(log_of(self.decays.precv, m)) * state + self.precv[m, 0:HALF].astype(F32)
         rows = pl.ds(pl.multiple_of(self.me * HALF, HALF), HALF)
         for k in (4, 3, 5, 2, 6, 1, 7):
             to = lax.rem(self.me + k, MEMBERS)
@@ -163,18 +166,21 @@
             self.all_of(exchange).wait_send()
 
 
-SCAN_BUFFERS = [
-    pltpu.VMEM((MEMBERS, PIECE, HW), BF16),
-    pltpu.VMEM((MEMBERS, PIECE, HW), BF16),
-    pltpu.VMEM((PIECE, HW), BF16),
-    pltpu.VMEM((GROUPS, PIECE, HW), BF16),
-    pltpu.VMEM((PIECE, HW), BF16),
-    pltpu.VMEM((NX, PIECE, HW), BF16),
-    pltpu.VMEM((MEMBERS, HALF, HW), BF16),
-    pltpu.VMEM((NH * HW, HW), BF16),
-    pltpu.SemaphoreType.DMA((8,)),
-]
-NB = len(SCAN_BUFFERS)
+def scan_buffers(length):
+    return [
+        pltpu.VMEM((MEMBERS, length, HW), BF16),
+        pltpu.VMEM((MEMBERS, length, HW), BF16),
+        pltpu.VMEM((length, HW), BF16),
+        pltpu.VMEM((GROUPS, length, HW), BF16),
+        pltpu.VMEM((length, HW), BF16),
+        pltpu.VMEM((NX, length, HW), BF16),
+        pltpu.VMEM((MEMBERS, HALF, HW), BF16),
+        pltpu.VMEM((NH * HW, HW), BF16),
+        pltpu.SemaphoreType.DMA((8,)),
+    ]
+
+
+NB = len(scan_buffers(HALF))
 
 
 def kernel(q_hbm, k_hbm, v_hbm, codes_hbm, w_hbm, og_hbm, mixed_out, qg_out, kg_out, vg_out, *scratch):
@@ -185,7 +191,8 @@
     seq, y = lax.axis_index("seq"), lax.axis_index("head")
     x, z, c = seq // (NZ * NC), lax.rem(seq, NZ * NC) // NC, lax.rem(seq, NC)
     place = (x, z, c, y)
-    fwd, bwd = Scan(place, False, fwd_refs), Scan(place, True, bwd_refs)
+    fwd = Scan(place, False, fwd_refs)
+    bwd = Scan(place, True, bwd_refs, fwd)
 
     codes_copy, k_copy, v_copy, og_copy, q_copy, w_copy = [
         pltpu.make_async_copy(src, dst, in_sem.at[i])
@@ -198,10 +205,11 @@
         return {"seq": seq, "head": lax.rem(y + NY + offset, NY)}
 
     barrier = pltpu.get_barrier_semaphore()
-    greeted = [fwd.member(lax.rem(fwd.me + k, MEMBERS)) for k in range(1, MEMBERS)]
+    greeted = [fwd.member(lax.rem(fwd.me + k, MEMBERS)) for k in (4, 3, 5, 2, 6)]
+    greeted += [row(k) for k in (2, -2, 1, -1)]
+    greeted += [fwd.member(lax.rem(fwd.me + k, MEMBERS)) for k in (1, 7)]
+    greeted += [fwd.device(lax.rem(x + k, NX), z, c) for k in (2, 1, 3)]
     greeted += [fwd.device(x, lax.rem(z + k * ZG, NZ), c) for k in range(1, GROUPS)]
-    greeted += [fwd.device(lax.rem(x + k, NX), z, c) for k in range(1, NX)]
-    greeted += [row(k) for k in (1, -1, 2, -2)]
     for where in greeted:
         pl.semaphore_signal(barrier, inc=1, device_id=where, device_id_type=MESH)
     for copy in (k_copy, v_copy, og_copy, q_copy, w_copy):
@@ -236,7 +244,16 @@
     with scope("wait_barrier"):
         og_copy.wait()
         pl.semaphore_wait(barrier, len(greeted))
-    top, bottom, every = slice(0, HALF), slice(HALF, TOK), slice(0, TOK)
+    every = slice(0, TOK)
+
+    def ways_of(parts):
+        cuts = [slice(i * HALF // parts, (i + 1) * HALF // parts) for i in range(2 * parts)]
+        return ((0, 1, cuts[:parts], cuts[parts:]), (1, -1, cuts[parts:], cuts[:parts]))
+
+    ways = ways_of(AG_PARTS)
+
+    def at(offset):
+        return lax.rem(y + NY + offset, NY)
 
     def ag_copy(owner, rows, i, where, src=None):
         src = ag.at[owner, rows] if src is None else src
@@ -246,12 +263,13 @@
     def ag_wait(i, owner, rows=every):
         ag_copy(owner, rows, i, row(1)).wait_recv()
 
-    def at(offset):
-        return lax.rem(y + NY + offset, NY)
-
-    for i, rows in ((1, top), (3, bottom)):
-        for j, sign in enumerate((1, -1)):
-            ag_copy(y, rows, i + j, row(2 * sign), og_ref.at[rows]).start()
+    def ag_index(step, j, i):
+        return 4 + (step * 2 + j) * 2 * AG_PARTS + i
+
+    for i in range(2 * AG_PARTS):
+        for j, sign, far, near in ways:
+            rows = (far + near)[i]
+            ag_copy(y, rows, ag_index(0, j, i), row(sign), og_ref.at[rows]).start()
     fwd.start_pieces()
 
     q_copy.wait()
@@ -267,8 +285,6 @@
         qrise_s[:, heads[h]] = (rise_s[h] * q_h.astype(F32)).astype(BF16)
         out_s[:, heads[h]] = nn(attn, v_h)
 
-    for j, sign in enumerate((1, -1)):
-        ag_copy(y, every, 5 + j, row(sign), og_ref).start()
     with scope("wait_w"):
         w_copy.wait()
 
@@ -280,32 +296,34 @@
     def add_grad(offset):
         grad_s[...] += nt(ag[at(offset)], w_cols(at(offset)))
 
+    for i in range(2 * AG_PARTS):
+        for j, sign, far, near in ways:
+            rows = (far + near)[i]
+            with scope("wait_ag1"):
+                ag_wait(ag_index(0, j, i), at(-sign), rows)
+            ag_copy(at(-sign), rows, ag_index(1, j, i), row(sign)).start()
     with scope("wait_pieces_fwd"):
         fwd.wait_pieces()
     fwd.start_groups()
-    for i, rows in ((1, top), (3, bottom)):
-        for j, sign in enumerate((1, -1)):
-            owner = at(-2 * sign)
+    for i in range(2 * AG_PARTS):
+        for j, sign, far, near in ways:
+            rows = (far + near)[i]
             with scope("wait_ag2"):
-                ag_wait(i + j, owner, rows)
-            if (rows == top) == (sign == 1):
-                ag_copy(owner, rows, 9, row(2 * sign)).start()
-            ag_copy(owner, rows, 7 + j, row(sign)).start()
-    add_grad(2)
-    add_grad(-2)
-    for j, sign in enumerate((1, -1)):
-        with scope("wait_ag1"):
-            ag_wait(5 + j, at(-sign))
-        add_grad(-sign)
+                ag_wait(ag_index(1, j, i), at(-2 * sign), rows)
+            if i < AG_PARTS:
+                ag_copy(at(-2 * sign), rows, 3, row(2 * sign)).start()
+            ag_copy(at(-2 * sign), rows, 1 + j, row(sign)).start()
+    for offset in (1, -1, 2, -2):
+        add_grad(offset)
     with scope("wait_groups_fwd"):
         fwd.wait_groups()
     fwd.start_planes()
-    for j, sign in enumerate((1, -1)):
+    for j, sign, far, near in ways:
         with scope("wait_ag3"):
-            ag_wait(7 + j, at(-3 * sign))
+            ag_wait(1 + j, at(-3 * sign))
         add_grad(-3 * sign)
     with scope("wait_ag4"):
-        ag_wait(9, at(4))
+        ag_wait(3, at(4))
     add_grad(4)
     for h in range(NH):
         last = jnp.broadcast_to(cum[TOK - 1:TOK, h:h + 1], (1, HW))
@@ -343,39 +361,54 @@
         return pltpu.make_async_remote_copy(rs_send.at[slot, rows], rs_recv.at[slot, rows], rs_sem.at[0], rs_sem.at[i],
                                             device_id=where, device_id_type=MESH)
 
-    ways = ((1, bottom, top), (-1, top, bottom))
-    for j, (sign, first, second) in enumerate(ways):
-        rs_send[j] = part(3 * sign).astype(BF16)
-        rs_copy(j, first, 1 + j, row(sign)).start()
-    rs_send[2] = part(4).astype(BF16)
-    for j, (sign, first, second) in enumerate(ways):
-        rs_copy(2, second, 3 + j, row(2 * sign)).start()
-        rs_copy(j, second, 3 + j, row(sign)).start()
-    for j, (sign, first, second) in enumerate(ways):
-        rs_send[3 + j] = part(sign).astype(BF16)
-        rs_copy(3 + j, every, 5, row(sign)).start()
-    onward = [part(2 * sign) for sign, _, _ in ways]
+    ways = ways_of(RS_PARTS)
+
+    def rs_index(left, j, i):
+        return 2 + ((left - 2) * 2 + j) * 2 * RS_PARTS + i
+
+    def rs_slot(left, j):
+        return 0 if left == 4 else 7 - 2 * left + j
+
+    def rs_on(left, i, parts):
+        for j, sign, far, near in ways:
+            rows, to = (near + far)[i], rs_slot(left, j)
+            total = parts[j][rows]
+            if left < 3 or i >= RS_PARTS:
+                came = rs_slot(left + 1, j)
+                with scope("wait_rs%d" % (left + 1)):
+                    rs_copy(came, rows, rs_index(left + 1, j, i), row(sign)).wait_recv()
+                total = total + rs_recv[came, rows].astype(F32)
+            rs_send[to, rows] = total.astype(BF16)
+            rs_copy(to, rows, 1 if left == 1 else rs_index(left, j, i), row(sign)).start()
+
+    rs_send[0] = part(4).astype(BF16)
+    for i in range(RS_PARTS):
+        for j, sign, far, near in ways:
+            rs_copy(0, far[i], rs_index(4, j, RS_PARTS + i), row(sign)).start()
+    three = [part(3 * sign) for _, sign, _, _ in ways]
+    for i in range(RS_PARTS):
+        rs_on(3, i, three)
+    two = [part(2 * sign) for _, sign, _, _ in ways]
+    one = [part(sign) for _, sign, _, _ in ways]
     own = part(0)
 
     with scope("wait_groups_bwd"):
         bwd.wait_groups()
     bwd.start_planes()
 
-    for j, (sign, first, second) in enumerate(ways):
-        with scope("wait_rs3"):
-            rs_copy(j, first, 1 + j, row(sign)).wait_recv()
-        rs_send[5 + j, first] = (onward[j][first] + rs_recv[j, first].astype(F32)).astype(BF16)
-        rs_copy(5 + j, first, 5, row(2 * sign)).start()
-    for j, (sign, first, second) in enumerate(ways):
-        with scope("wait_rs4"):
-            rs_copy(j, every, 3 + j, row(sign)).wait_recv()
-        rs_send[5 + j, second] = (onward[j][second] + rs_recv[j, second].astype(F32)
-                                  + rs_recv[2, second].astype(F32)).astype(BF16)
-        rs_copy(5 + j, second, 5, row(2 * sign)).start()
-
-    with scope("wait_planes_bwd"):
-        bwd.wait_planes()
-    bwd.start_back()
+    for i in range(RS_PARTS):
+        rs_on(3, RS_PARTS + i, three)
+    for i in range(RS_PARTS):
+        rs_on(2, i, two)
+    for i in range(RS_PARTS):
+        if i == RS_PARTS // 2:
+            with scope("wait_planes_bwd"):
+                bwd.wait_planes()
+            bwd.start_back()
+        rs_on(2, RS_PARTS + i, two)
+
+    for i in range(2 * RS_PARTS):
+        rs_on(1, i, one)
 
     for h in range(NH):
         g_rise = (rise_s[h] * grad_s[:, heads[h]].astype(BF16).astype(F32)).astype(BF16)
@@ -392,11 +425,11 @@
     out_copies[2].start()
     out_copies[3].start()
 
-    with scope("wait_rs2"):
-        pltpu.make_async_remote_copy(rs_send.at[3:7], rs_recv.at[3:7], rs_sem.at[0], rs_sem.at[5],
+    with scope("wait_rs1"):
+        pltpu.make_async_remote_copy(rs_send.at[5:7], rs_recv.at[5:7], rs_sem.at[0], rs_sem.at[1],
                                      device_id=row(1), device_id_type=MESH).wait_recv()
     total = own
-    for slot in (3, 4, 5, 6):
+    for slot in (5, 6):
         total = total + rs_recv[slot].astype(F32)
     mixed_ref[...] = total.astype(BF16)
     out_copies[0].start()
@@ -439,7 +472,7 @@
         ),
         in_specs=[pl.BlockSpec(memory_space=pltpu.HBM)] * 6,
         out_specs=(pl.BlockSpec(memory_space=pl.ANY),) * 4,
-        scratch_shapes=SCAN_BUFFERS + SCAN_BUFFERS + [
+        scratch_shapes=scan_buffers(PIECE) + scan_buffers(HALF) + [
             pltpu.VMEM((TOK, wide), BF16),
             pltpu.VMEM((TOK, wide), BF16),
             pltpu.VMEM((TOK, wide), BF16),
@@ -448,10 +481,10 @@
             pltpu.VMEM((TOK, COLS), BF16),
             pltpu.SemaphoreType.DMA((6,)),
             pltpu.VMEM((NY, TOK, COLS), BF16),
-            pltpu.SemaphoreType.DMA((10,)),
+            pltpu.SemaphoreType.DMA((4 + 8 * AG_PARTS,)),
             pltpu.VMEM((7, TOK, COLS), BF16),
             pltpu.VMEM((7, TOK, COLS), BF16),
-            pltpu.SemaphoreType.DMA((6,)),
+            pltpu.SemaphoreType.DMA((2 + 12 * RS_PARTS,)),
             pltpu.VMEM((NH, TOK, TOK), BF16),
             pltpu.VMEM((TOK, wide), BF16),
             pltpu.VMEM((TOK, wide), BF16),

time: 53.9 us -> 52.1 us (0.967); the launches traced: 53.8 us -> 51.1 us
  Pallas kernels: 53.2 us -> 50.5 us
    pallas_call x1, Pallas kernels: 52.4 us -> 49.7 us  [local(): pl.pallas_call(kernel, out_shape=(pltpu.VMEM((TOK, COLS), BF16), pltpu.VM...]
where the time goes in v3:
time: 52.1 us; the launch traced here: 51.1 us
  Pallas kernels  50.5 us (97%)
  between operations  0.64 us (1%)
    pallas_call x1, Pallas kernels, local(): pl.pallas_call(kernel, out_shape=(pltpu.VMEM((TOK, COLS), BF16), pltpu.VM...  49.7 us

profile of v3, /device:TPU:1, one launch (start us, length us, event | category | flops | bytes accessed | tf_op | source)
XLA Modules:
  0.0 51.1 jit_solution(2883225446401666695)
XLA Ops:
  0.6 49.7 %linear_attention.1 = (bf16[128,384]{1,0:T(8,128)(2,1)S(1)}, bf16[128,512]{1,0:T(8,128)(2,1)S(1)}, bf16[128,512]{1,0:T(8,128)(2,1)S(1)}, bf16[128,512]{1,0:T(8,128)(2,1)S(1)}) custom-call(bf16[128,512]{1,0:T(8,128)(2,1)} %q_hbm.1, bf16[128,512]{1,0:T(8,128)(2,1)} %k_hbm.1, bf16[128,512]{1,0:T(8,128)(2,1)} %v_hbm.1, s32[4,128]{1,0:T(4,128)} %bitcast.1, ...), custom_call_target="tpu_custom_call" | custom-call | tf_op jit(solution)/shard_map/linear_attention/pallas_call | solution.py:465
  50.3 0.8 %store.1 = (bf16[128,384]{1,0:T(8,128)(2,1)}, bf16[128,512]{1,0:T(8,128)(2,1)}, bf16[128,512]{1,0:T(8,128)(2,1)}, bf16[128,512]{1,0:T(8,128)(2,1)}) custom-call(bf16[128,384]{1,0:T(8,128)(2,1)S(1)} %get-tuple-element.8.refs_0_, bf16[128,512]{1,0:T(8,128)(2,1)S(1)} %get-tuple-element.9.refs_1_, bf16[128,512]{1,0:T(8,128)(2,1)S(1)} %get-tuple-element.10.refs_2_, ...), custom_call_target="tpu_custom_call" | custom-call | tf_op jit(solution)/shard_map/store/pallas_call | solution.py:509

commit v4 on v3

--- a/solution.py
+++ b/solution.py
@@ -19,10 +19,9 @@
 NH = 4
 COLS = 384
 HALF = HW // 2
-PIECE = HALF + 16
 SCALE = 1.0 / HW
 AG_PARTS = 2
-RS_PARTS = 2
+RS_PARTS = 4
 TRACE = False
 
 
@@ -40,21 +39,6 @@
 
 def tn(a, b):
     return lax.dot_general(a, b, (((0,), (0,)), ((), ())), preferred_element_type=F32)
-
-
-def log_tile(log_total):
-    high = log_total.astype(BF16)
-    rest = log_total - high.astype(F32)
-    mid = rest.astype(BF16)
-    low = (rest - mid.astype(F32)).astype(BF16)
-    row = lax.broadcasted_iota(jnp.int32, (16, HW), 0)
-    parts = [jnp.broadcast_to(part.astype(F32), (16, HW)) for part in (high, mid, low)]
-    tile = jnp.where(row == 0, parts[0], jnp.where(row == 1, parts[1], jnp.where(row == 2, parts[2], 0.0)))
-    return tile.astype(BF16)
-
-
-def log_of(ref, m):
-    return jnp.sum(ref[m, HALF:PIECE].astype(F32), axis=0, keepdims=True)
 
 
 class Scan:
@@ -62,7 +46,9 @@
         self.x, self.z, self.c, self.y = place
         self.reverse = reverse
         self.decays = other or self
-        (self.psend, self.precv, self.gsend, self.zrecv, self.xsend, self.xrecv, self.bsend, self.brecv, self.sem) = refs
+        (self.psend, self.precv, self.gsend, self.zrecv, self.xsend, self.xrecv, self.bsend, self.brecv, self.sem) = refs[:9]
+        if other is None:
+            self.lsend, self.lrecv, self.lgsend, self.lzrecv, self.lxsend, self.lxrecv, self.lsem = refs[9:]
         self.group = self.z // ZG
         self.me = lax.rem(self.z, ZG) * NC + self.c
 
@@ -81,21 +67,35 @@
                self.brecv.at[0:(MEMBERS - 1) * HALF])[exchange]
         return self.copy(ref, ref, exchange, self.member(lax.rem(self.me + 1, MEMBERS)))
 
-    def put(self, head, summary, log_total):
+    def put(self, head, summary, log_total=None):
         data = summary.astype(BF16)
         for half in range(2):
-            self.psend[2 * head + half, 0:HALF, :] = data[half * HALF:(half + 1) * HALF]
-            if self.decays is self:
-                self.psend[2 * head + half, HALF:PIECE, :] = log_tile(log_total)
+            self.psend[2 * head + half] = data[half * HALF:(half + 1) * HALF]
+        if self.decays is self:
+            self.lsend[head] = log_total
+
+    def log_copy(self, src, dst, exchange, where):
+        return pltpu.make_async_remote_copy(src, dst, self.lsem.at[2 * exchange], self.lsem.at[2 * exchange + 1],
+                                            device_id=where, device_id_type=MESH)
+
+    def all_logs(self, exchange):
+        ref = (self.lrecv.at[0:MEMBERS - 1], self.lzrecv.at[0:GROUPS - 1], self.lxrecv.at[0:NX - 1])[exchange]
+        return self.log_copy(ref, ref, exchange, self.member(lax.rem(self.me + 1, MEMBERS)))
 
     def start_pieces(self):
         for k in (4, 3, 5, 2, 6, 1, 7):
             to = lax.rem(self.me + k, MEMBERS)
             self.copy(self.psend.at[to], self.precv.at[self.me], 0, self.member(to)).start()
+            if self.decays is self:
+                self.log_copy(self.lsend.at[to // 2], self.lrecv.at[self.me], 0, self.member(to)).start()
         self.precv[self.me] = self.psend[self.me]
+        if self.decays is self:
+            self.lrecv[self.me] = self.lsend[self.me // 2]
 
     def wait_pieces(self):
         self.all_of(0).wait_recv()
+        if self.decays is self:
+            self.all_logs(0).wait_recv()
 
     def order(self, count):
         return reversed(range(count)) if self.reverse else range(count)
@@ -104,17 +104,22 @@
         total = jnp.zeros((HALF, HW), F32)
         log_total = jnp.zeros((1, HW), F32)
         for m in self.order(MEMBERS):
-            log_m = log_of(self.decays.precv, m)
-            total = jnp.exp(log_m) * total + self.precv[m, 0:HALF].astype(F32)
+            log_m = self.decays.lrecv[m]
+            total = jnp.exp(log_m) * total + self.precv[m].astype(F32)
             log_total = log_total + log_m
-        self.gsend[0:HALF, :] = total.astype(BF16)
-        if self.decays is self:
-            self.gsend[HALF:PIECE, :] = log_tile(log_total)
+        self.gsend[...] = total.astype(BF16)
+        if self.decays is self:
+            self.lgsend[...] = log_total
         for k in range(1, GROUPS):
             to = lax.rem(self.group + k, GROUPS)
             self.copy(self.gsend, self.zrecv.at[self.group], 1,
                       self.device(self.x, to * ZG + lax.rem(self.z, ZG), self.c)).start()
+            if self.decays is self:
+                self.log_copy(self.lgsend, self.lzrecv.at[self.group], 1,
+                              self.device(self.x, to * ZG + lax.rem(self.z, ZG), self.c)).start()
         self.zrecv[self.group] = self.gsend[...]
+        if self.decays is self:
+            self.lzrecv[self.group] = self.lgsend[...]
 
     def prefix(self, recv, decays, count, place):
         before = jnp.zeros((HALF, HW), F32)
@@ -124,34 +129,42 @@
         for m in self.order(count):
             before = jnp.where(place == m, total, before)
             log_before = jnp.where(place == m, log_total, log_before)
-            log_m = log_of(decays, m)
-            total = jnp.exp(log_m) * total + recv[m, 0:HALF].astype(F32)
+            log_m = decays[m]
+            total = jnp.exp(log_m) * total + recv[m].astype(F32)
             log_total = log_total + log_m
         return before, log_before, total, log_total
 
     def wait_groups(self):
         self.all_of(1).wait_recv()
+        if self.decays is self:
+            self.all_logs(1).wait_recv()
 
     def start_planes(self):
         self.before, self.log_before, total, log_total = self.prefix(
-            self.zrecv, self.decays.zrecv, GROUPS, self.group)
-        self.xsend[0:HALF, :] = total.astype(BF16)
-        if self.decays is self:
-            self.xsend[HALF:PIECE, :] = log_tile(log_total)
+            self.zrecv, self.decays.lzrecv, GROUPS, self.group)
+        self.xsend[...] = total.astype(BF16)
+        if self.decays is self:
+            self.lxsend[...] = log_total
         for k in (2, 1, 3):
             to = lax.rem(self.x + k, NX)
             self.copy(self.xsend, self.xrecv.at[self.x], 2, self.device(to, self.z, self.c)).start()
+            if self.decays is self:
+                self.log_copy(self.lxsend, self.lxrecv.at[self.x], 2, self.device(to, self.z, self.c)).start()
         self.xrecv[self.x] = self.xsend[...]
+        if self.decays is self:
+            self.lxrecv[self.x] = self.lxsend[...]
 
     def wait_planes(self):
         self.all_of(2).wait_recv()
+        if self.decays is self:
+            self.all_logs(2).wait_recv()
 
     def start_back(self):
-        entering, _, _, _ = self.prefix(self.xrecv, self.decays.xrecv, NX, self.x)
+        entering, _, _, _ = self.prefix(self.xrecv, self.decays.lxrecv, NX, self.x)
         state = jnp.exp(self.log_before) * entering + self.before
         for m in self.order(MEMBERS):
             self.bsend[m] = state.astype(BF16)
-            state = jnp.exp(log_of(self.decays.precv, m)) * state + self.precv[m, 0:HALF].astype(F32)
+            state = jnp.exp(self.decays.lrecv[m]) * state + self.precv[m].astype(F32)
         rows = pl.ds(pl.multiple_of(self.me * HALF, HALF), HALF)
         for k in (4, 3, 5, 2, 6, 1, 7):
             to = lax.rem(self.me + k, MEMBERS)
@@ -164,30 +177,38 @@
     def finish(self):
         for exchange in range(4):
             self.all_of(exchange).wait_send()
-
-
-def scan_buffers(length):
-    return [
-        pltpu.VMEM((MEMBERS, length, HW), BF16),
-        pltpu.VMEM((MEMBERS, length, HW), BF16),
-        pltpu.VMEM((length, HW), BF16),
-        pltpu.VMEM((GROUPS, length, HW), BF16),
-        pltpu.VMEM((length, HW), BF16),
-        pltpu.VMEM((NX, length, HW), BF16),
-        pltpu.VMEM((MEMBERS, HALF, HW), BF16),
-        pltpu.VMEM((NH * HW, HW), BF16),
-        pltpu.SemaphoreType.DMA((8,)),
-    ]
-
-
-NB = len(scan_buffers(HALF))
-
-
-def kernel(q_hbm, k_hbm, v_hbm, codes_hbm, w_hbm, og_hbm, mixed_out, qg_out, kg_out, vg_out, *scratch):
-    fwd_refs, bwd_refs, rest = scratch[:NB], scratch[NB:2 * NB], scratch[2 * NB:]
+            if self.decays is self and exchange < 3:
+                self.all_logs(exchange).wait_send()
+
+
+STATE_BUFFERS = [
+    pltpu.VMEM((MEMBERS, HALF, HW), BF16),
+    pltpu.VMEM((MEMBERS, HALF, HW), BF16),
+    pltpu.VMEM((HALF, HW), BF16),
+    pltpu.VMEM((GROUPS, HALF, HW), BF16),
+    pltpu.VMEM((HALF, HW), BF16),
+    pltpu.VMEM((NX, HALF, HW), BF16),
+    pltpu.VMEM((MEMBERS, HALF, HW), BF16),
+    pltpu.VMEM((NH * HW, HW), BF16),
+    pltpu.SemaphoreType.DMA((8,)),
+]
+LOG_BUFFERS = [
+    pltpu.VMEM((NH, 1, HW), F32),
+    pltpu.VMEM((MEMBERS, 1, HW), F32),
+    pltpu.VMEM((1, HW), F32),
+    pltpu.VMEM((GROUPS, 1, HW), F32),
+    pltpu.VMEM((1, HW), F32),
+    pltpu.VMEM((NX, 1, HW), F32),
+    pltpu.SemaphoreType.DMA((6,)),
+]
+NF = len(STATE_BUFFERS) + len(LOG_BUFFERS)
+NB = NF + len(STATE_BUFFERS)
+
+
+def kernel(q_hbm, k_hbm, v_hbm, codes_hbm, w_hbm, og_hbm, mixed_ref, qg_ref, kg_ref, vg_ref, *scratch):
+    fwd_refs, bwd_refs, rest = scratch[:NF], scratch[NF:NB], scratch[NB:]
     (q_ref, k_ref, v_ref, codes_ref, w_ref, og_ref, in_sem, ag, ag_sem, rs_send, rs_recv, rs_sem,
-     attn_s, kfall_s, qrise_s, grad_s, out_s, qg_s, kg_s, vg_s, rise_s, fall_s,
-     mixed_ref, qg_ref, kg_ref, vg_ref, out_sem) = rest
+     attn_s, kfall_s, qrise_s, grad_s, out_s, qg_s, kg_s, vg_s, rise_s, fall_s, vfall_s) = rest
     seq, y = lax.axis_index("seq"), lax.axis_index("head")
     x, z, c = seq // (NZ * NC), lax.rem(seq, NZ * NC) // NC, lax.rem(seq, NC)
     place = (x, z, c, y)
@@ -244,6 +265,7 @@
     with scope("wait_barrier"):
         og_copy.wait()
         pl.semaphore_wait(barrier, len(greeted))
+    fwd.start_pieces()
     every = slice(0, TOK)
 
     def ways_of(parts):
@@ -270,7 +292,6 @@
         for j, sign, far, near in ways:
             rows = (far + near)[i]
             ag_copy(y, rows, ag_index(0, j, i), row(sign), og_ref.at[rows]).start()
-    fwd.start_pieces()
 
     q_copy.wait()
     masks = []
@@ -326,8 +347,7 @@
         ag_wait(3, at(4))
     add_grad(4)
     for h in range(NH):
-        last = jnp.broadcast_to(cum[TOK - 1:TOK, h:h + 1], (1, HW))
-        bwd.put(h, tn(qrise_s[:, heads[h]], grad_s[:, heads[h]].astype(BF16)), last)
+        bwd.put(h, tn(qrise_s[:, heads[h]], grad_s[:, heads[h]].astype(BF16)))
     bwd.start_pieces()
     with scope("wait_planes_fwd"):
         fwd.wait_planes()
@@ -340,6 +360,7 @@
         qg_s[:, heads[h]] = nn(pmat, k_h)
         kg_s[:, heads[h]] = tn(pmat, q_h)
         vg_s[:, heads[h]] = tn(attn_s[h], g_h)
+        vfall_s[:, heads[h]] = (fall_s[h] * v_ref[:, heads[h]].astype(F32)).astype(BF16)
 
     with scope("wait_pieces_bwd"):
         bwd.wait_pieces()
@@ -354,9 +375,6 @@
     def part(offset):
         return nn(attn_out, w_cols(lax.rem(y + NY + offset, NY)))
 
-    out_copies = [pltpu.make_async_copy(src, dst, out_sem.at[i]) for i, (src, dst) in enumerate(
-        ((mixed_ref, mixed_out), (qg_ref, qg_out), (kg_ref, kg_out), (vg_ref, vg_out)))]
-
     def rs_copy(slot, rows, i, where):
         return pltpu.make_async_remote_copy(rs_send.at[slot, rows], rs_recv.at[slot, rows], rs_sem.at[0], rs_sem.at[i],
                                             device_id=where, device_id_type=MESH)
@@ -369,25 +387,31 @@
     def rs_slot(left, j):
         return 0 if left == 4 else 7 - 2 * left + j
 
+    def rs_wait(slot, rows, i):
+        with scope("wait_rs%d" % slot):
+            rs_copy(slot, rows, i, row(1)).wait_recv()
+        return rs_recv[slot, rows].astype(F32)
+
     def rs_on(left, i, parts):
         for j, sign, far, near in ways:
-            rows, to = (near + far)[i], rs_slot(left, j)
-            total = parts[j][rows]
-            if left < 3 or i >= RS_PARTS:
-                came = rs_slot(left + 1, j)
-                with scope("wait_rs%d" % (left + 1)):
-                    rs_copy(came, rows, rs_index(left + 1, j, i), row(sign)).wait_recv()
-                total = total + rs_recv[came, rows].astype(F32)
+            rows, to, came = (near + far)[i], rs_slot(left, j), rs_slot(left + 1, j)
+            total = parts[j][rows] + rs_wait(came, rows, rs_index(left + 1, j, i))
+            if left == 2 and i >= RS_PARTS:
+                total = total + rs_wait(0, rows, rs_index(4, j, i))
             rs_send[to, rows] = total.astype(BF16)
             rs_copy(to, rows, 1 if left == 1 else rs_index(left, j, i), row(sign)).start()
 
     rs_send[0] = part(4).astype(BF16)
     for i in range(RS_PARTS):
         for j, sign, far, near in ways:
-            rs_copy(0, far[i], rs_index(4, j, RS_PARTS + i), row(sign)).start()
-    three = [part(3 * sign) for _, sign, _, _ in ways]
+            rs_copy(0, far[i], rs_index(4, j, RS_PARTS + i), row(2 * sign)).start()
+    for j, sign, far, near in ways:
+        rs_send[1 + j] = part(3 * sign).astype(BF16)
+        for i in range(RS_PARTS):
+            rs_copy(1 + j, far[i], rs_index(3, j, RS_PARTS + i), row(sign)).start()
     for i in range(RS_PARTS):
-        rs_on(3, i, three)
+        for j, sign, far, near in ways:
+            rs_copy(1 + j, near[i], rs_index(3, j, i), row(sign)).start()
     two = [part(2 * sign) for _, sign, _, _ in ways]
     one = [part(sign) for _, sign, _, _ in ways]
     own = part(0)
@@ -397,33 +421,27 @@
     bwd.start_planes()
 
     for i in range(RS_PARTS):
-        rs_on(3, RS_PARTS + i, three)
+        rs_on(2, RS_PARTS + i, two)
     for i in range(RS_PARTS):
         rs_on(2, i, two)
+    with scope("wait_planes_bwd"):
+        bwd.wait_planes()
+    bwd.start_back()
     for i in range(RS_PARTS):
-        if i == RS_PARTS // 2:
-            with scope("wait_planes_bwd"):
-                bwd.wait_planes()
-            bwd.start_back()
-        rs_on(2, RS_PARTS + i, two)
-
-    for i in range(2 * RS_PARTS):
+        rs_on(1, RS_PARTS + i, one)
+    for i in range(RS_PARTS):
         rs_on(1, i, one)
 
     for h in range(NH):
         g_rise = (rise_s[h] * grad_s[:, heads[h]].astype(BF16).astype(F32)).astype(BF16)
         qg_ref[:, heads[h]] = (qg_s[:, heads[h]] + nt(g_rise, fwd.brecv[heads[h], :])).astype(BF16)
-    out_copies[1].start()
 
     with scope("wait_back_bwd"):
         bwd.wait_back()
     for h in range(NH):
         carry = bwd.brecv[heads[h], :]
-        v_fall = (fall_s[h] * v_ref[:, heads[h]].astype(F32)).astype(BF16)
-        kg_ref[:, heads[h]] = (kg_s[:, heads[h]] + nt(v_fall, carry)).astype(BF16)
+        kg_ref[:, heads[h]] = (kg_s[:, heads[h]] + nt(vfall_s[:, heads[h]], carry)).astype(BF16)
         vg_ref[:, heads[h]] = (vg_s[:, heads[h]] + nn(kfall_s[:, heads[h]], carry)).astype(BF16)
-    out_copies[2].start()
-    out_copies[3].start()
 
     with scope("wait_rs1"):
         pltpu.make_async_remote_copy(rs_send.at[5:7], rs_recv.at[5:7], rs_sem.at[0], rs_sem.at[1],
@@ -432,7 +450,6 @@
     for slot in (5, 6):
         total = total + rs_recv[slot].astype(F32)
     mixed_ref[...] = total.astype(BF16)
-    out_copies[0].start()
 
     with scope("wait_sends"):
         fwd.finish()
@@ -441,9 +458,6 @@
                                      device_id=row(1), device_id_type=MESH).wait_send()
         pltpu.make_async_remote_copy(rs_send, rs_recv, rs_sem.at[0], rs_sem.at[1],
                                      device_id=row(1), device_id_type=MESH).wait_send()
-    with scope("wait_out"):
-        for copy in out_copies:
-            copy.wait()
 
 
 def store(*refs):
@@ -471,8 +485,8 @@
             pltpu.VMEM((TOK, wide), BF16),
         ),
         in_specs=[pl.BlockSpec(memory_space=pltpu.HBM)] * 6,
-        out_specs=(pl.BlockSpec(memory_space=pl.ANY),) * 4,
-        scratch_shapes=scan_buffers(PIECE) + scan_buffers(HALF) + [
+        out_specs=(vmem,) * 4,
+        scratch_shapes=STATE_BUFFERS + LOG_BUFFERS + STATE_BUFFERS + [
             pltpu.VMEM((TOK, wide), BF16),
             pltpu.VMEM((TOK, wide), BF16),
             pltpu.VMEM((TOK, wide), BF16),
@@ -495,11 +509,7 @@
             pltpu.VMEM((TOK, wide), F32),
             pltpu.VMEM((NH, TOK, HW), F32),
             pltpu.VMEM((NH, TOK, HW), F32),
-            pltpu.VMEM((TOK, COLS), BF16),
-            pltpu.VMEM((TOK, wide), BF16),
-            pltpu.VMEM((TOK, wide), BF16),
-            pltpu.VMEM((TOK, wide), BF16),
-            pltpu.SemaphoreType.DMA((4,)),
+            pltpu.VMEM((TOK, wide), BF16),
         ],
         name="linear_attention",
         compiler_params=pltpu.CompilerParams(

time: 52.1 us -> 51.1 us (0.981)
  Pallas kernels: 50.5 us -> 49.6 us
    pallas_call x1, Pallas kernels: 49.7 us -> 48.8 us  [local(): pl.pallas_call(kernel, out_shape=(pltpu.VMEM((TOK, COLS), BF16), pltpu.VM...]
where the time goes in v4:
time: 51.1 us; the launch traced here: 50.3 us
  Pallas kernels  49.6 us (97%)
  between operations  0.64 us (1%)
    pallas_call x1, Pallas kernels, local(): pl.pallas_call(kernel, out_shape=(pltpu.VMEM((TOK, COLS), BF16), pltpu.VM...  48.8 us

profile of v4, /device:TPU:1, one launch (start us, length us, event | category | flops | bytes accessed | tf_op | source)
XLA Modules:
  0.0 50.3 jit_solution(2375898360337992284)
XLA Ops:
  0.6 48.8 %linear_attention.1 = (bf16[128,384]{1,0:T(8,128)(2,1)S(1)}, bf16[128,512]{1,0:T(8,128)(2,1)S(1)}, bf16[128,512]{1,0:T(8,128)(2,1)S(1)}, bf16[128,512]{1,0:T(8,128)(2,1)S(1)}) custom-call(bf16[128,512]{1,0:T(8,128)(2,1)} %q_hbm.1, bf16[128,512]{1,0:T(8,128)(2,1)} %k_hbm.1, bf16[128,512]{1,0:T(8,128)(2,1)} %v_hbm.1, s32[4,128]{1,0:T(4,128)} %bitcast.1, ...), custom_call_target="tpu_custom_call" | custom-call | tf_op jit(solution)/shard_map/linear_attention/pallas_call | solution.py:479
  49.5 0.8 %store.1 = (bf16[128,384]{1,0:T(8,128)(2,1)}, bf16[128,512]{1,0:T(8,128)(2,1)}, bf16[128,512]{1,0:T(8,128)(2,1)}, bf16[128,512]{1,0:T(8,128)(2,1)}) custom-call(bf16[128,384]{1,0:T(8,128)(2,1)S(1)} %get-tuple-element.8.refs_0_, bf16[128,512]{1,0:T(8,128)(2,1)S(1)} %get-tuple-element.9.refs_1_, bf16[128,512]{1,0:T(8,128)(2,1)S(1)} %get-tuple-element.10.refs_2_, ...), custom_call_target="tpu_custom_call" | custom-call | tf_op jit(solution)/shard_map/store/pallas_call | solution.py:519

commit v5 on v4

--- a/solution.py
+++ b/solution.py
@@ -409,10 +409,10 @@
         rs_send[1 + j] = part(3 * sign).astype(BF16)
         for i in range(RS_PARTS):
             rs_copy(1 + j, far[i], rs_index(3, j, RS_PARTS + i), row(sign)).start()
+    two = [part(2 * sign) for _, sign, _, _ in ways]
     for i in range(RS_PARTS):
         for j, sign, far, near in ways:
             rs_copy(1 + j, near[i], rs_index(3, j, i), row(sign)).start()
-    two = [part(2 * sign) for _, sign, _, _ in ways]
     one = [part(sign) for _, sign, _, _ in ways]
     own = part(0)
 

time: 51.1 us -> 51.1 us (level)
  no operation moved by 1% of the time
where the time goes in v5:
time: 51.1 us; the launch traced here: 50.3 us
  Pallas kernels  49.6 us (97%)
  between operations  0.64 us (1%)
    pallas_call x1, Pallas kernels, local(): pl.pallas_call(kernel, out_shape=(pltpu.VMEM((TOK, COLS), BF16), pltpu.VM...  48.8 us

profile of v5, /device:TPU:1, one launch (start us, length us, event | category | flops | bytes accessed | tf_op | source)
XLA Modules:
  0.0 50.3 jit_solution(5057864213512591386)
XLA Ops:
  0.6 48.8 %linear_attention.1 = (bf16[128,384]{1,0:T(8,128)(2,1)S(1)}, bf16[128,512]{1,0:T(8,128)(2,1)S(1)}, bf16[128,512]{1,0:T(8,128)(2,1)S(1)}, bf16[128,512]{1,0:T(8,128)(2,1)S(1)}) custom-call(bf16[128,512]{1,0:T(8,128)(2,1)} %q_hbm.1, bf16[128,512]{1,0:T(8,128)(2,1)} %k_hbm.1, bf16[128,512]{1,0:T(8,128)(2,1)} %v_hbm.1, s32[4,128]{1,0:T(4,128)} %bitcast.1, ...), custom_call_target="tpu_custom_call" | custom-call | tf_op jit(solution)/shard_map/linear_attention/pallas_call | solution.py:479
  49.5 0.8 %store.1 = (bf16[128,384]{1,0:T(8,128)(2,1)}, bf16[128,512]{1,0:T(8,128)(2,1)}, bf16[128,512]{1,0:T(8,128)(2,1)}, bf16[128,512]{1,0:T(8,128)(2,1)}) custom-call(bf16[128,384]{1,0:T(8,128)(2,1)S(1)} %get-tuple-element.8.refs_0_, bf16[128,512]{1,0:T(8,128)(2,1)S(1)} %get-tuple-element.9.refs_1_, bf16[128,512]{1,0:T(8,128)(2,1)S(1)} %get-tuple-element.10.refs_2_, ...), custom_call_target="tpu_custom_call" | custom-call | tf_op jit(solution)/shard_map/store/pallas_call | solution.py:519
